TPU v7x, 128 devices: a whole 4x4x4 slice. The times are simulated.
128 devices in a mesh: head: 16 (over z, y), tok: 8 (over x, core).
Axes of the slice: x: 4, y: 4, z: 4, core: 2. Of those that a mesh axis runs over, the one named last changes fastest.
Arguments:
- queries: bfloat16 [2048, 8192], P('tok', 'head'), may hold values from -6 to 6
- cache: bfloat16 [4, 4096, 256], P(None, 'tok'), may hold values from -6 to 6
- new_kv: bfloat16 [4, 2048, 256], P(None, 'tok'), may hold values from -6 to 6
- q_gain: float32 [128], replicated, may hold values from 0.5 to 2.2
- k_gain: float32 [128], replicated, may hold values from 0.5 to 2.2
- out_weight: bfloat16 [8192, 4096], P('head'), may hold values from -0.5 to 0.5
- residual: bfloat16 [2048, 4096], P(('tok', 'head')), may hold values from -3 to 3
- norm_gain: float32 [4096], replicated, may hold values from 0.25 to 1.75
- expert_ids: int32 [2048, 8], P(('tok', 'head')), may hold values from 0 to 127, all different within a row; in each aligned block of 16 rows (0 to 15, 16 to 31, ...) at most 2 rows name the same one
- combine_weight: bfloat16 [2048, 8], P(('tok', 'head')), may hold values from 0.049804688 to 0.5
- prefix_len: int32 [1], replicated, may hold values from 2048 to 4096
- w_gate_up: bfloat16 [128, 4096, 1536], P(('head', 'tok')), may hold values from -0.09375 to 0.09375
- w_down: bfloat16 [128, 768, 4096], P(('head', 'tok')), may hold values from -0.21875 to 0.21875
Outputs:
- layer_out: bfloat16 [2048, 4096], P(('tok', 'head'))
Inputs may be any that keep to these rules, and one draw needn't show every extreme that they name: `expert_ids`: in each aligned block of 16 rows (the rows of one device) no expert is named by more than 2 rows, and some expert reaches 2.
All inputs are finite; a program needn't handle non-finite values.
Results may differ from a plain program's by a relative error of at most 0.022.
Values may be sent and summed in bfloat16 or wider, within the bound.
No kernel may reach another device: no remote copies, remote signals or barrier semaphores. Data moves between devices by JAX's collectives and lax.ppermute only.
A program may use at most 128 MiB of HBM per device.

v0:
```python
import functools
import math

import jax
import jax.numpy as jnp
from jax import lax
from jax.experimental import pallas as pl
from jax.experimental.pallas import tpu as pltpu
from jax.sharding import Mesh
from jax.sharding import PartitionSpec as P

HEADS = 64
KV_HEADS = 4
HD = 128
WIDTH = 4096
ROWS = 16
QROWS = 256
QHEADS = 4
CACHE_ROWS = 512
SHARD = CACHE_ROWS + QROWS
PART = SHARD // 2
GROUPS = 16
EXPERTS = 128
SLOTS = 2
CHUNKS = 8
PIECE = WIDTH // CHUNKS
LINES = CHUNKS * SLOTS
FFE = 768
GROUP = 16
GROUP_LINES = GROUP * LINES
EPSILON = 1e-06
SCALE = math.log2(math.e) / math.sqrt(HD)
MB = 1 << 20

F32 = jnp.float32
BF16 = jnp.bfloat16

VMEM = functools.partial(pl.BlockSpec, memory_space=pltpu.VMEM)
SMEM = functools.partial(pl.BlockSpec, memory_space=pltpu.SMEM)
HBM = functools.partial(pl.BlockSpec, memory_space=pltpu.HBM)


def params(limit):
    return pltpu.CompilerParams(vmem_limit_bytes=limit * MB)


def rms_scale(values, gain):
    mean_square = jnp.mean(values * values, axis=-1, keepdims=True)
    return values * lax.rsqrt(mean_square + EPSILON) * gain


def shift(step):
    return [(i, (i + step) % 4) for i in range(4)]


def prep_kernel(place_ref, cache_ref, new_ref, gain_ref, first, second, cache, new, gain, sems):
    head = place_ref[1]
    copies = (
        pltpu.make_async_copy(gain_ref, gain, sems.at[0]),
        pltpu.make_async_copy(cache_ref.at[head], cache, sems.at[1]),
        pltpu.make_async_copy(new_ref.at[head], new, sems.at[2]),
    )
    for copy in copies:
        copy.start()
    for copy in copies:
        copy.wait()
    rest = CACHE_ROWS - PART
    for ref, start, out_ref, there, rows in (
        (cache, 0, first, 0, PART),
        (cache, PART, second, 0, rest),
        (new, 0, second, rest, QROWS),
    ):
        held = ref[pl.ds(start, rows), :]
        keys = rms_scale(held[:, :HD].astype(F32), gain[...]).astype(BF16)
        out_ref[pl.ds(there, rows), :HD] = keys
        out_ref[pl.ds(there, rows), HD:] = held[:, HD:]


def prep(place, cache, new_kv, k_gain):
    return pl.pallas_call(
        prep_kernel,
        in_specs=[SMEM(), HBM(), HBM(), HBM()],
        out_specs=[VMEM()] * 2,
        out_shape=[jax.ShapeDtypeStruct((PART, 2 * HD), BF16)] * 2,
        scratch_shapes=[
            pltpu.VMEM((CACHE_ROWS, 2 * HD), BF16),
            pltpu.VMEM((QROWS, 2 * HD), BF16),
            pltpu.VMEM((1, HD), F32),
            pltpu.SemaphoreType.DMA((3,)),
        ],
        compiler_params=params(8),
    )(place, cache, new_kv, k_gain)


def join(first, second, whole):
    whole[pl.ds(0, PART), :] = first[...]
    whole[pl.ds(PART, PART), :] = second[...]


def add_block(ref, start, rows, qn, acc, total, mask=None):
    keys = ref[pl.ds(start, rows), :HD]
    values = ref[pl.ds(start, rows), HD:]
    scores = lax.dot_general(qn[...], keys, (((1,), (1,)), ((), ())), preferred_element_type=F32)
    weights = jnp.exp2(scores * SCALE)
    if mask is not None:
        weights = jnp.where(mask, weights, 0.0)
    part = weights[:, :HD]
    for i in range(1, rows // HD):
        part = part + weights[:, i * HD : (i + 1) * HD]
    total[...] += part
    acc[...] += jnp.dot(weights.astype(BF16), values, preferred_element_type=F32)


def add_shard(place_ref, who, distance, ref, qn, acc, total):
    limit, x, c = place_ref[0], place_ref[3], place_ref[4]
    tok = x * 2 + lax.rem(c + who, 2)
    owner = lax.rem(x + 4 - distance, 4) * 2 + c
    visible = limit - owner * CACHE_ROWS
    whole, earlier = visible >= CACHE_ROWS, owner < tok

    @pl.when(whole & earlier)
    def _():
        add_block(ref, 0, SHARD, qn, acc, total)

    @pl.when(whole & jnp.logical_not(earlier))
    def _():
        add_block(ref, 0, CACHE_ROWS, qn, acc, total)

    @pl.when((visible > 0) & (visible < CACHE_ROWS))
    def _():
        key = lax.broadcasted_iota(jnp.int32, (QHEADS * QROWS, CACHE_ROWS), 1)
        add_block(ref, 0, CACHE_ROWS, qn, acc, total, key < visible)

    @pl.when(jnp.logical_not(whole) & earlier)
    def _():
        add_block(ref, CACHE_ROWS, QROWS, qn, acc, total)


STATE = jax.ShapeDtypeStruct((2, QHEADS * QROWS, HD), F32)


def near_kernel(place_ref, qn, first, second, weight_ref, acc, total, weight, shard, sem):
    copy = pltpu.make_async_copy(weight_ref, weight, sem)
    copy.start()
    join(first, second, shard)
    acc[...] = jnp.zeros_like(acc)
    total[...] = jnp.zeros_like(total)

    @pl.loop(0, 2)
    def _(who):
        add_shard(place_ref, who, 0, shard, qn.at[who], acc.at[who], total.at[who])

    key = lax.broadcasted_iota(jnp.int32, (QHEADS * QROWS, QROWS), 1)
    query = lax.broadcasted_iota(jnp.int32, (QHEADS * QROWS, QROWS), 0)
    mask = key <= lax.rem(query, QROWS)
    add_block(shard, CACHE_ROWS, QROWS, qn.at[0], acc.at[0], total.at[0], mask)
    copy.wait()


def attend_near(place, qn, first, second, weight):
    return pl.pallas_call(
        near_kernel,
        in_specs=[SMEM()] + [VMEM()] * 3 + [HBM()],
        out_specs=[VMEM()] * 3,
        out_shape=[STATE, STATE, jax.ShapeDtypeStruct(weight.shape, BF16)],
        scratch_shapes=[pltpu.VMEM((SHARD, 2 * HD), BF16), pltpu.SemaphoreType.DMA],
        compiler_params=params(20),
    )(place, qn, first, second, weight)


def middle_kernel(place_ref, qn, acc_ref, total_ref, *refs):
    parts, (acc, total, shards) = refs[:4], refs[4:]
    acc[...] = acc_ref[...]
    total[...] = total_ref[...]
    join(parts[0], parts[1], shards.at[0])
    join(parts[2], parts[3], shards.at[1])

    @pl.loop(0, 4)
    def _(step):
        who, side = lax.div(step, 2), lax.rem(step, 2)
        distance = 1 + 2 * side
        add_shard(
            place_ref, who, distance, shards.at[side], qn.at[who], acc.at[who], total.at[who]
        )


def attend_middle(place, qn, acc, total, parts):
    return pl.pallas_call(
        middle_kernel,
        in_specs=[SMEM()] + [VMEM()] * 7,
        out_specs=[VMEM()] * 2,
        out_shape=[STATE] * 2,
        scratch_shapes=[pltpu.VMEM((2, SHARD, 2 * HD), BF16)],
        compiler_params=params(16),
    )(place, qn, acc, total, *parts)


def far_kernel(who, place_ref, qn, acc_ref, total_ref, first, second, out_ref, acc, total, shard):
    acc[...] = acc_ref[who]
    total[...] = total_ref[who]
    join(first, second, shard)
    add_shard(place_ref, who, 2, shard, qn.at[who], acc, total)
    out_ref[:, :HD] = acc[...]
    out_ref[:, HD:] = total[...]


def attend_far(who, place, qn, acc, total, first, second):
    return pl.pallas_call(
        functools.partial(far_kernel, who),
        in_specs=[SMEM()] + [VMEM()] * 5,
        out_specs=VMEM(),
        out_shape=jax.ShapeDtypeStruct((QHEADS * QROWS, 2 * HD), F32),
        scratch_shapes=[
            pltpu.VMEM((QHEADS * QROWS, HD), F32),
            pltpu.VMEM((QHEADS * QROWS, HD), F32),
            pltpu.VMEM((SHARD, 2 * HD), BF16),
        ],
        compiler_params=params(16),
    )(place, qn, acc, total, first, second)


def project_kernel(place_ref, own_ref, other_ref, weight, *refs):
    outs, attn, ordered = refs[:4], refs[4], refs[5]
    z, y, c = place_ref[1], place_ref[2], place_ref[4]
    for h in range(QHEADS):
        at = pl.ds(h * QROWS, QROWS)
        both = own_ref[at, :] + other_ref[at, :]
        whole = jnp.sum(both[:, HD:], axis=1, keepdims=True)
        attn[:, h * HD : (h + 1) * HD] = (both[:, :HD] / whole).astype(BF16)
    for k in range(4):
        for i in range(4):
            over_y = i * 4 + lax.rem(y + k, 4)
            over_z = lax.rem(z + k, 4) * 4 + i
            group = jnp.where(c == 0, over_y, over_z)
            start = pl.multiple_of(group * ROWS, ROWS)
            ordered[pl.ds((k * 4 + i) * ROWS, ROWS), :] = attn[pl.ds(start, ROWS), :]
    for n in range(8):
        part = slice(n * 512, (n + 1) * 512)
        product = jnp.dot(ordered[...], weight[:, part], preferred_element_type=F32)
        product = product.astype(BF16).reshape(GROUPS, ROWS, 512)
        for k in range(4):
            outs[k][:, :, part] = product[k * 4 : (k + 1) * 4]


def project(place, own, other, weight):
    return pl.pallas_call(
        project_kernel,
        in_specs=[SMEM()] + [VMEM()] * 3,
        out_specs=[VMEM()] * 4,
        out_shape=[jax.ShapeDtypeStruct((4, ROWS, WIDTH), BF16)] * 4,
        scratch_shapes=[pltpu.VMEM((QROWS, QHEADS * HD), BF16)] * 2,
        compiler_params=params(16),
    )(place, own, other, weight)


def around(level, step):
    pairs = []
    for z in range(4):
        for y in range(4):
            for x in range(4):
                for c in range(2):
                    to_z, to_y = (z, (y + step) % 4) if c == level else ((z + step) % 4, y)
                    pairs.append((((z * 4 + y) * 4 + x) * 2 + c, ((to_z * 4 + to_y) * 4 + x) * 2 + c))
    return pairs


def sum_kernel(place_ref, *refs):
    parts, outs, held = refs[:4], refs[4:8], refs[8]
    mine = jnp.where(place_ref[4] == 0, place_ref[1], place_ref[2])
    for i in range(4):
        value = parts[0][i].astype(F32)
        for other in parts[1:]:
            value = value + other[i].astype(F32)
        held[i] = value.astype(BF16)
    for k in range(4):
        outs[k][...] = held[lax.rem(mine + k, 4)]


def first_sum(place, parts):
    return pl.pallas_call(
        sum_kernel,
        in_specs=[SMEM()] + [VMEM()] * 4,
        out_specs=[VMEM()] * 4,
        out_shape=[jax.ShapeDtypeStruct((ROWS, WIDTH), BF16)] * 4,
        scratch_shapes=[pltpu.VMEM((4, ROWS, WIDTH), BF16)],
        compiler_params=params(12),
    )(place, *parts)


def route_kernel(
    ids_hbm, weights_hbm, q_ref, gain_ref, other_ref, placing_ref, mixing_ref, qn,
    ids_ref, weights_ref, queries, gain, sems,
):
    pairs = ((gain_ref, gain), (q_ref, queries), (ids_hbm, ids_ref), (weights_hbm, weights_ref))
    copies = [pltpu.make_async_copy(a, b, sems.at[i]) for i, (a, b) in enumerate(pairs)]
    for copy in copies:
        copy.start()
    for copy in copies:
        copy.wait()
    square = (EXPERTS, EXPERTS)
    expert = lax.broadcasted_iota(jnp.int32, square, 0)
    lane = lax.broadcasted_iota(jnp.int32, square, 1)
    row = lax.broadcasted_iota(jnp.int32, (ROWS, EXPERTS), 0)
    spread = lax.broadcasted_iota(jnp.int32, (ROWS, EXPERTS), 1) % ROWS == row
    spread = jnp.where(spread, 1.0, 0.0).astype(BF16)
    ids = jnp.dot(ids_ref[...].astype(F32).astype(BF16), spread, preferred_element_type=F32)
    ids = ids.astype(jnp.int32)
    weights = jnp.dot(weights_ref[...], spread, preferred_element_type=F32)
    named = jnp.zeros(square, F32)
    value = jnp.zeros(square, F32)
    for k in range(8):
        hit = expert == ids[k : k + 1, :]
        named = jnp.where(hit, 1.0, named)
        value = jnp.where(hit, weights[k : k + 1, :], value)
    earlier = (expert // ROWS == lane // ROWS) & (expert < lane)
    before = jnp.dot(
        named.astype(BF16), jnp.where(earlier, 1.0, 0.0).astype(BF16), preferred_element_type=F32
    )
    lines = (EXPERTS * LINES, EXPERTS)
    line = lax.broadcasted_iota(jnp.int32, lines, 0)
    column = lax.broadcasted_iota(jnp.int32, lines, 1)
    same = (line // SLOTS) % CHUNKS == column // ROWS
    of_expert = line // LINES == column
    for out_ref, held in ((placing_ref, named), (mixing_ref, value)):
        table = jnp.zeros(lines, F32)
        for s in range(SLOTS):
            pick = jnp.where(of_expert & (line % SLOTS == s), 1.0, 0.0).astype(BF16)
            slot = jnp.where(before == s, held, 0.0).astype(BF16)
            table = table + jnp.dot(pick, slot, preferred_element_type=F32)
        out_ref[...] = jnp.where(same, table, 0.0).astype(BF16)
    for who, ref in enumerate((queries, other_ref)):
        for h in range(QHEADS):
            head = ref[:, h * HD : (h + 1) * HD].astype(F32)
            qn[who, pl.ds(h * QROWS, QROWS), :] = rms_scale(head, gain[...]).astype(BF16)


def route(expert_ids, combine_weight, queries, q_gain, other):
    return pl.pallas_call(
        route_kernel,
        in_specs=[HBM()] * 4 + [VMEM()],
        out_specs=[VMEM()] * 3,
        out_shape=[jax.ShapeDtypeStruct((EXPERTS * LINES, EXPERTS), BF16)] * 2
        + [jax.ShapeDtypeStruct((2, QHEADS * QROWS, HD), BF16)],
        scratch_shapes=[
            pltpu.VMEM((8, ROWS), jnp.int32),
            pltpu.VMEM((8, ROWS), BF16),
            pltpu.VMEM((QROWS, QHEADS * HD), BF16),
            pltpu.VMEM((1, HD), F32),
            pltpu.SemaphoreType.DMA((4,)),
        ],
        compiler_params=params(16),
    )(expert_ids, combine_weight, queries, q_gain, other)


def dispatch_kernel(*refs):
    parts, refs = refs[:4], refs[4:]
    residual_ref, gain_ref, placing_ref, hidden_ref, out_ref, pieces = refs
    for n in range(8):
        columns = slice(n * 512, (n + 1) * 512)
        value = residual_ref[:, columns].astype(F32)
        for part in parts:
            value = value + part[:, columns].astype(F32)
        hidden_ref[:, columns] = value
    normed = rms_scale(hidden_ref[...], gain_ref[...]).astype(BF16)
    for k in range(CHUNKS):
        pieces[pl.ds(k * ROWS, ROWS), :] = normed[:, k * PIECE : (k + 1) * PIECE]
    for g in range(8):
        lines = jnp.dot(
            placing_ref[pl.ds(g * GROUP_LINES, GROUP_LINES), :],
            pieces[...],
            preferred_element_type=F32,
        )
        out_ref[pl.ds(g * GROUP, GROUP)] = lines.astype(BF16).reshape(GROUP, LINES, PIECE)


def dispatch(parts, residual, norm_gain, placing):
    return pl.pallas_call(
        dispatch_kernel,
        in_specs=[VMEM()] * 7,
        out_specs=[VMEM()] * 2,
        out_shape=[
            jax.ShapeDtypeStruct((ROWS, WIDTH), F32),
            jax.ShapeDtypeStruct((EXPERTS, LINES, PIECE), BF16),
        ],
        scratch_shapes=[pltpu.VMEM((EXPERTS, PIECE), BF16)],
        compiler_params=params(12),
    )(*parts, residual, norm_gain, placing)


def expert_kernel(
    lines_ref, up_ref, down_hbm, out_ref, rows, both, active, back, down_ref, sem
):
    copy = pltpu.make_async_copy(down_hbm, down_ref, sem)
    copy.start()
    size = (GROUP_LINES, GROUP_LINES)
    first = lax.broadcasted_iota(jnp.int32, size, 0)
    second = lax.broadcasted_iota(jnp.int32, size, 1)
    span = GROUP * SLOTS

    def held(by_chunk, by_source):
        source = (by_chunk % span) // SLOTS
        line = source * LINES + (by_chunk // span) * SLOTS + by_chunk % SLOTS
        return jnp.where(line == by_source, 1.0, 0.0).astype(BF16)

    gather, scatter = held(first, second), held(second, first)
    for g in range(8):
        group = lines_ref[pl.ds(g * GROUP, GROUP)].reshape(GROUP_LINES, PIECE)
        sorted_lines = jnp.dot(gather, group, preferred_element_type=F32).astype(BF16)
        for k in range(CHUNKS):
            rows[pl.ds(g * span, span), k * PIECE : (k + 1) * PIECE] = sorted_lines[
                k * span : (k + 1) * span, :
            ]
    for n in range(2 * FFE // 256):
        columns = slice(n * 256, (n + 1) * 256)
        both[:, columns] = jnp.dot(rows[...], up_ref[:, columns], preferred_element_type=F32)
    gate = both[:, :FFE]
    active[...] = (gate * jax.nn.sigmoid(gate) * both[:, FFE:]).astype(BF16)
    copy.wait()
    for k in range(CHUNKS):
        columns = slice(k * PIECE, (k + 1) * PIECE)
        down = jnp.dot(active[...], down_ref[:, columns], preferred_element_type=F32)
        down = down.astype(BF16)
        for g in range(8):
            back[g, pl.ds(k * span, span), :] = down[g * span : (g + 1) * span, :]
    for g in range(8):
        lines = jnp.dot(scatter, back[g], preferred_element_type=F32).astype(BF16)
        out_ref[pl.ds(g * GROUP, GROUP)] = lines.reshape(GROUP, LINES, PIECE)


def experts(lines, gate_up, down):
    return pl.pallas_call(
        expert_kernel,
        in_specs=[VMEM(), VMEM(), HBM()],
        out_specs=VMEM(),
        out_shape=jax.ShapeDtypeStruct((EXPERTS, LINES, PIECE), BF16),
        scratch_shapes=[
            pltpu.VMEM((EXPERTS * SLOTS, WIDTH), BF16),
            pltpu.VMEM((EXPERTS * SLOTS, 2 * FFE), F32),
            pltpu.VMEM((EXPERTS * SLOTS, FFE), BF16),
            pltpu.VMEM((8, GROUP_LINES, PIECE), BF16),
            pltpu.VMEM((FFE, WIDTH), BF16),
            pltpu.SemaphoreType.DMA,
        ],
        compiler_params=params(24),
    )(lines, gate_up, down)


def combine_kernel(lines_ref, mixing_ref, hidden_ref, out_ref):
    lines = lines_ref[...].reshape(EXPERTS * LINES, PIECE)
    mixed = lax.dot_general(
        mixing_ref[...], lines, (((0,), (0,)), ((), ())), preferred_element_type=F32
    )
    for k in range(CHUNKS):
        columns = slice(k * PIECE, (k + 1) * PIECE)
        value = hidden_ref[:, columns] + mixed[k * ROWS : (k + 1) * ROWS, :]
        out_ref[:, columns] = value.astype(BF16)


def combine(lines, mixing, hidden):
    return pl.pallas_call(
        combine_kernel,
        in_specs=[VMEM()] * 3,
        out_specs=VMEM(),
        out_shape=jax.ShapeDtypeStruct((ROWS, WIDTH), BF16),
        compiler_params=params(12),
    )(lines, mixing, hidden)


def per_device(
    queries,
    cache,
    new_kv,
    q_gain,
    k_gain,
    out_weight,
    residual,
    norm_gain,
    expert_ids,
    combine_weight,
    prefix_len,
    w_gate_up,
    w_down,
):
    z, y, x, c = (lax.axis_index(name).astype(jnp.int32) for name in ("z", "y", "x", "c"))
    place = jnp.stack([prefix_len[0], z, y, x, c])
    held = functools.partial(pltpu.with_memory_space_constraint, memory_space=pltpu.HBM)
    swap = functools.partial(lax.ppermute, axis_name="c", perm=[(0, 1), (1, 0)])
    other = swap(queries)
    left, right = shift(1), shift(3)
    own = prep(place, held(cache), held(new_kv), held(k_gain.reshape(1, HD)))
    first_left, second_right = lax.ppermute(own[0], "x", left), lax.ppermute(own[1], "x", right)
    second_left, first_right = lax.ppermute(own[1], "x", left), lax.ppermute(own[0], "x", right)
    placing, mixing, qn = route(
        held(expert_ids.T), held(combine_weight.T), held(queries), held(q_gain.reshape(1, HD)), other
    )
    first_left, second_right, placing, mixing, qn = lax.optimization_barrier(
        (first_left, second_right, placing, mixing, qn)
    )
    first, second = lax.ppermute(first_left, "x", left), lax.ppermute(second_right, "x", right)
    acc, total, weight = attend_near(place, qn, *own, held(out_weight))
    parts = (first_left, second_left, first_right, second_right)
    acc, total = attend_middle(place, qn, acc, total, parts)
    far = attend_far(1, place, qn, acc, total, first, second)
    far, acc, total = lax.optimization_barrier((far, acc, total))
    mine = attend_far(0, place, qn, acc, total, first, second)
    everyone = ("z", "y", "x", "c")
    parts = project(place, mine, swap(far), weight)
    for level in range(2):
        if level:
            parts = first_sum(place, parts)
        moved = [lax.ppermute(parts[k], everyone, around(level, k)) for k in (1, 2, 3)]
        parts = [parts[0], *moved]
    hidden, lines = dispatch(parts, residual, norm_gain.reshape(1, WIDTH), placing)
    lines = lax.all_to_all(lines, everyone, split_axis=0, concat_axis=0, tiled=True)
    lines = experts(lines, w_gate_up[0], w_down[0])
    lines = lax.all_to_all(lines, everyone, split_axis=0, concat_axis=0, tiled=True)
    return combine(lines, mixing, hidden)


def solution(mesh):
    fine = Mesh(mesh.devices.reshape(4, 4, 4, 2), ("z", "y", "x", "c"))
    head, tok = ("z", "y"), ("x", "c")
    placed = (
        P(tok, head),
        P(None, tok, None),
        P(None, tok, None),
        P(),
        P(),
        P(head, None),
        P(tok + head, None),
        P(),
        P(tok + head, None),
        P(tok + head, None),
        P(),
        P(head + tok, None, None),
        P(head + tok, None, None),
    )
    return jax.shard_map(
        per_device, mesh=fine, in_specs=placed, out_specs=P(tok + head, None), check_vma=False
    )
```

profile of v0, /device:TPU:1, one launch (start us, length us, event | category | flops | bytes accessed | tf_op | source)
XLA Modules:
  0.0 139.9 jit_solution(8585037905690328103)
XLA Ops:
  0.0 1.4 %collective-permute-start.2 = (bf16[256,512]{1,0:T(8,128)(2,1)}, bf16[256,512]{1,0:T(8,128)(2,1)S(1)}, u32[]{:S(2)}, u32[]{:S(2)}) collective-permute-start(bf16[256,512]{1,0:T(8,128)(2,1)} %q_ref.1), channel_id=1, source_target_pairs={{0,1},{1,0},{2,3},{3,2},{4,5},{5,4},{6,7},{7,6},{8,9},{9,8},{10,11... | collective-permute-start | bytes 786440 | tf_op jit(solution)/shard_map/ppermute | solution.py:488
  2.2 1.8 %shard_map.127 = (bf16[384,256]{1,0:T(8,128)(2,1)S(1)}, bf16[384,256]{1,0:T(8,128)(2,1)S(1)}) custom-call(s32[5]{0:T(128)S(1)} %stack.19.place_ref, bf16[4,512,256]{2,1,0:T(8,128)(2,1)} %cache_ref.1, bf16[4,256,256]{2,1,0:T(8,128)(2,1)} %new_ref.1, f32[1,128]{1,0:T(1,128)} %bitcast.20), custom_call_target="tpu_custom_call" | custom-call | tf_op jit(solution)/shard_map/pallas_call | solution.py:80
  3.9 1.4 collective-permute-start
  5.3 1.4 collective-permute-start.1
  6.8 2.6 %collective-permute-start.4 = (bf16[384,256]{1,0:T(8,128)(2,1)S(1)}, bf16[384,256]{1,0:T(8,128)(2,1)S(1)}, u32[]{:S(2)}, u32[]{:S(2)}) collective-permute-start(bf16[384,256]{1,0:T(8,128)(2,1)S(1)} %get-tuple-element.33.first), channel_id=1, source_target_pairs={{0,6},{2,0},{4,2},{6,4},{1,7},{3,1},{5,3},{7,5},{8,14},{10,8},{12,... | collective-permute-start | bytes 589832 | tf_op jit(solution)/shard_map/ppermute | solution.py:492
  9.3 2.2 %shard_map.128 = (bf16[2048,128]{1,0:T(8,128)(2,1)S(1)}, bf16[2048,128]{1,0:T(8,128)(2,1)S(1)}, bf16[2,1024,128]{2,1,0:T(8,128)(2,1)S(1)}) custom-call(s32[8,16]{1,0:T(8,128)} %bitcast.18, bf16[8,16]{1,0:T(8,128)(2,1)} %bitcast.19, bf16[256,512]{1,0:T(8,128)(2,1)} %q_ref.1, f32[1,128]{1,0:T(1,128)} %bitcast.21, ...), custom_call_target="tpu_custom_call" | custom-call | tf_op jit(solution)/shard_map/pallas_call | solution.py:338
  12.7 1.7 %collective-permute-start.6 = (bf16[384,256]{1,0:T(8,128)(2,1)S(1)}, bf16[384,256]{1,0:T(8,128)(2,1)S(1)}, u32[]{:S(2)}, u32[]{:S(2)}) collective-permute-start(bf16[384,256]{1,0:T(8,128)(2,1)S(1)} %collective-permute-done.1.refs_3_), channel_id=1, source_target_pairs={{0,6},{2,0},{4,2},{6,4},{1,7},{3,1},{5,3},{7,5},{8,14},{10,8},{12,... | collective-permute-start | bytes 589832 | tf_op jit(solution)/shard_map/ppermute | solution.py:499
  14.4 2.8 %shard_map.129 = (f32[2,1024,128]{2,1,0:T(8,128)S(1)}, f32[2,1024,128]{2,1,0:T(8,128)S(1)}, bf16[512,4096]{1,0:T(8,128)(2,1)S(1)}) custom-call(s32[5]{0:T(128)S(1)} %stack.19.place_ref, bf16[2,1024,128]{2,1,0:T(8,128)(2,1)S(1)} %get-tuple-element.38.qn, bf16[384,256]{1,0:T(8,128)(2,1)S(1)} %get-tuple-element.33.first, ...), custom_call_target="tpu_custom_call" | custom-call | tf_op jit(solution)/shard_map/pallas_call | solution.py:161
  17.2 2.3 %shard_map.130 = (f32[2,1024,128]{2,1,0:T(8,128)S(1)}, f32[2,1024,128]{2,1,0:T(8,128)S(1)}) custom-call(s32[5]{0:T(128)S(1)} %stack.19.place_ref, bf16[2,1024,128]{2,1,0:T(8,128)(2,1)S(1)} %get-tuple-element.38.qn, f32[2,1024,128]{2,1,0:T(8,128)S(1)} %get-tuple-element.39.acc_ref, f32[2,1024,128]{2,1,0:T(8,128)S(1)} %get-tuple-element.40.total_ref, ...), custom_call_target="tpu_custom_call" | custom-call | tf_op jit(solution)/shard_map/pallas_call | solution.py:188
  20.5 3.2 %collective-permute-start.7 = (f32[1024,256]{1,0:T(8,128)S(1)}, f32[1024,256]{1,0:T(8,128)S(1)}, u32[]{:S(2)}, u32[]{:S(2)}) collective-permute-start(f32[1024,256]{1,0:T(8,128)S(1)} %shard_map.131), channel_id=1, source_target_pairs={{0,1},{1,0},{2,3},{3,2},{4,5},{5,4},{6,7},{7,6},{8,9},{9,8},{10,11... | collective-permute-start | bytes 3145736 | tf_op jit(solution)/shard_map/ppermute | solution.py:507
  24.4 1.6 %collective-permute-done.7.other_ref = f32[1024,256]{1,0:T(8,128)S(1)} collective-permute-done((f32[1024,256]{1,0:T(8,128)S(1)}, f32[1024,256]{1,0:T(8,128)S(1)}, u32[]{:S(2)}, u32[]{:S(2)}) %collective-permute-start.7) | collective-permute-done | bytes 1048608 | tf_op jit(solution)/shard_map/ppermute | solution.py:507
  26.0 2.0 %shard_map.133 = (bf16[4,16,4096]{2,1,0:T(8,128)(2,1)S(1)}, bf16[4,16,4096]{2,1,0:T(8,128)(2,1)S(1)}, bf16[4,16,4096]{2,1,0:T(8,128)(2,1)S(1)}, bf16[4,16,4096]{2,1,0:T(8,128)(2,1)S(1)}) custom-call(s32[5]{0:T(128)S(1)} %stack.19.place_ref, f32[1024,256]{1,0:T(8,128)S(1)} %shard_map.132.own_ref, f32[1024,256]{1,0:T(8,128)S(1)} %collective-permute-done.7.other_ref, ...), custom_call_target="tpu_custom_call" | custom-call | tf_op jit(solution)/shard_map/pallas_call | solution.py:246
  28.0 3.8 %collective-permute-start.10 = (bf16[4,16,4096]{2,1,0:T(8,128)(2,1)S(1)}, bf16[4,16,4096]{2,1,0:T(8,128)(2,1)S(1)}, u32[]{:S(2)}, u32[]{:S(2)}) collective-permute-start(bf16[4,16,4096]{2,1,0:T(8,128)(2,1)S(1)} %get-tuple-element.52), channel_id=1, source_target_pairs={{0,24},{1,97},{2,26},{3,99},{4,28},{5,101},{6,30},{7,103},{8,0},{9... | collective-permute-start | bytes 1572872 | tf_op jit(solution)/shard_map/ppermute | solution.py:511
  31.8 1.3 collective-permute-start.9
  33.1 10.4 %collective-permute-done.10.refs_3_ = bf16[4,16,4096]{2,1,0:T(8,128)(2,1)S(1)} collective-permute-done((bf16[4,16,4096]{2,1,0:T(8,128)(2,1)S(1)}, bf16[4,16,4096]{2,1,0:T(8,128)(2,1)S(1)}, u32[]{:S(2)}, u32[]{:S(2)}) %collective-permute-start.10) | collective-permute-done | bytes 524320 | tf_op jit(solution)/shard_map/ppermute | solution.py:511
  43.6 3.4 %collective-permute-done.8.refs_1_ = bf16[4,16,4096]{2,1,0:T(8,128)(2,1)S(1)} collective-permute-done((bf16[4,16,4096]{2,1,0:T(8,128)(2,1)S(1)}, bf16[4,16,4096]{2,1,0:T(8,128)(2,1)S(1)}, u32[]{:S(2)}, u32[]{:S(2)}) %collective-permute-start.8) | collective-permute-done | bytes 524320 | tf_op jit(solution)/shard_map/ppermute | solution.py:511
  47.9 1.1 collective-permute-start.11
  49.0 2.6 %collective-permute-start.12 = (bf16[16,4096]{1,0:T(8,128)(2,1)S(1)}, bf16[16,4096]{1,0:T(8,128)(2,1)S(1)}, u32[]{:S(2)}, u32[]{:S(2)}) collective-permute-start(bf16[16,4096]{1,0:T(8,128)(2,1)S(1)} %get-tuple-element.55), channel_id=1, source_target_pairs={{0,64},{1,17},{2,66},{3,19},{4,68},{5,21},{6,70},{7,23},{8,72},{9,... | collective-permute-start | bytes 393224 | tf_op jit(solution)/shard_map/ppermute | solution.py:511
  51.6 1.1 collective-permute-start.13
  53.0 2.3 %collective-permute-done.12.refs_2_ = bf16[16,4096]{1,0:T(8,128)(2,1)S(1)} collective-permute-done((bf16[16,4096]{1,0:T(8,128)(2,1)S(1)}, bf16[16,4096]{1,0:T(8,128)(2,1)S(1)}, u32[]{:S(2)}, u32[]{:S(2)}) %collective-permute-start.12) | collective-permute-done | bytes 131104 | tf_op jit(solution)/shard_map/ppermute | solution.py:511
  56.3 41.2 %all_to_all.10.lines_ref = bf16[128,16,512]{2,1,0:T(8,128)(2,1)S(1)} all-to-all(bf16[128,16,512]{2,1,0:T(8,128)(2,1)S(1)} %get-tuple-element.58), channel_id=1, replica_groups=mesh['z'=4,'y'=4,'x'=4,'c'=2] {'z','y','x','c'}, dimensions={0} | all-to-all | bytes 4194304 | tf_op jit(solution)/shard_map/all_to_all | solution.py:514
  97.6 6.8 %shard_map.136 = bf16[128,16,512]{2,1,0:T(8,128)(2,1)S(1)} custom-call(bf16[128,16,512]{2,1,0:T(8,128)(2,1)S(1)} %all_to_all.10.lines_ref, bf16[4096,1536]{1,0:T(8,128)(2,1)S(1)} %bitcast.13, bf16[768,4096]{1,0:T(8,128)(2,1)S(1)} %bitcast.16), custom_call_target="tpu_custom_call" | custom-call | tf_op jit(solution)/shard_map/pallas_call | solution.py:431
  104.4 34.4 %all_to_all.11.lines_ref = bf16[128,16,512]{2,1,0:T(8,128)(2,1)S(1)} all-to-all(bf16[128,16,512]{2,1,0:T(8,128)(2,1)S(1)} %shard_map.136), channel_id=1, replica_groups=mesh['z'=4,'y'=4,'x'=4,'c'=2] {'z','y','x','c'}, dimensions={0} | all-to-all | bytes 4194304 | tf_op jit(solution)/shard_map/all_to_all | solution.py:516
  138.8 1.1 shard_map.137
  (34 shorter events, 5.2 us)
Async XLA Ops:
  0.0 9.3 %collective-permute-start.2 = (bf16[256,512]{1,0:T(8,128)(2,1)}, bf16[256,512]{1,0:T(8,128)(2,1)S(1)}, u32[]{:S(2)}, u32[]{:S(2)}) collective-permute-start(bf16[256,512]{1,0:T(8,128)(2,1)} %q_ref.1), channel_id=1, source_target_pairs={{0,1},{1,0},{2,3},{3,2},{4,5},{5,4},{6,7},{7,6},{8,9},{9,8},{10,11... | collective-permute-start | bytes 786440 | tf_op jit(solution)/shard_map/ppermute | solution.py:488
  3.9 7.8 %collective-permute-start = (bf16[384,256]{1,0:T(8,128)(2,1)S(1)}, bf16[384,256]{1,0:T(8,128)(2,1)S(1)}, u32[]{:S(2)}, u32[]{:S(2)}) collective-permute-start(bf16[384,256]{1,0:T(8,128)(2,1)S(1)} %get-tuple-element.33.first), channel_id=1, source_target_pairs={{0,2},{2,4},{4,6},{6,0},{1,3},{3,5},{5,7},{7,1},{8,10},{10,12},{12... | collective-permute-start | bytes 589832 | tf_op jit(solution)/shard_map/ppermute | solution.py:491
  5.3 6.5 %collective-permute-start.1 = (bf16[384,256]{1,0:T(8,128)(2,1)S(1)}, bf16[384,256]{1,0:T(8,128)(2,1)S(1)}, u32[]{:S(2)}, u32[]{:S(2)}) collective-permute-start(bf16[384,256]{1,0:T(8,128)(2,1)S(1)} %get-tuple-element.34.second), channel_id=1, source_target_pairs={{0,6},{2,0},{4,2},{6,4},{1,7},{3,1},{5,3},{7,5},{8,14},{10,8},{12,... | collective-permute-start | bytes 589832 | tf_op jit(solution)/shard_map/ppermute | solution.py:491
  6.7 10.5 %collective-permute-start.3 = (bf16[384,256]{1,0:T(8,128)(2,1)S(1)}, bf16[384,256]{1,0:T(8,128)(2,1)S(1)}, u32[]{:S(2)}, u32[]{:S(2)}) collective-permute-start(bf16[384,256]{1,0:T(8,128)(2,1)S(1)} %get-tuple-element.34.second), channel_id=1, source_target_pairs={{0,2},{2,4},{4,6},{6,0},{1,3},{3,5},{5,7},{7,1},{8,10},{10,12},{12... | collective-permute-start | bytes 589832 | tf_op jit(solution)/shard_map/ppermute | solution.py:492
  6.8 10.4 %collective-permute-start.4 = (bf16[384,256]{1,0:T(8,128)(2,1)S(1)}, bf16[384,256]{1,0:T(8,128)(2,1)S(1)}, u32[]{:S(2)}, u32[]{:S(2)}) collective-permute-start(bf16[384,256]{1,0:T(8,128)(2,1)S(1)} %get-tuple-element.33.first), channel_id=1, source_target_pairs={{0,6},{2,0},{4,2},{6,4},{1,7},{3,1},{5,3},{7,5},{8,14},{10,8},{12,... | collective-permute-start | bytes 589832 | tf_op jit(solution)/shard_map/ppermute | solution.py:492
  11.7 7.8 %collective-permute-start.5 = (bf16[384,256]{1,0:T(8,128)(2,1)S(1)}, bf16[384,256]{1,0:T(8,128)(2,1)S(1)}, u32[]{:S(2)}, u32[]{:S(2)}) collective-permute-start(bf16[384,256]{1,0:T(8,128)(2,1)S(1)} %collective-permute-done.refs_0_), channel_id=1, source_target_pairs={{0,2},{2,4},{4,6},{6,0},{1,3},{3,5},{5,7},{7,1},{8,10},{10,12},{12... | collective-permute-start | bytes 589832 | tf_op jit(solution)/shard_map/ppermute | solution.py:499
  12.7 6.8 %collective-permute-start.6 = (bf16[384,256]{1,0:T(8,128)(2,1)S(1)}, bf16[384,256]{1,0:T(8,128)(2,1)S(1)}, u32[]{:S(2)}, u32[]{:S(2)}) collective-permute-start(bf16[384,256]{1,0:T(8,128)(2,1)S(1)} %collective-permute-done.1.refs_3_), channel_id=1, source_target_pairs={{0,6},{2,0},{4,2},{6,4},{1,7},{3,1},{5,3},{7,5},{8,14},{10,8},{12,... | collective-permute-start | bytes 589832 | tf_op jit(solution)/shard_map/ppermute | solution.py:499
  17.2 80.3 %slice-start = ((s8[12582912]{0:T(1024)(128)(4,1)}), s8[4194304]{0:T(1024)(128)(4,1)S(1)}, s32[]{:S(2)}) async-start(s8[12582912]{0:T(1024)(128)(4,1)} %bitcast.11), calls=%async_computation.2 | async-start | bytes 8388608
  19.5 78.0 %slice-start.3 = ((s8[6291456]{0:T(1024)(128)(4,1)}), s8[4194304]{0:T(1024)(128)(4,1)S(1)}, s32[]{:S(2)}) async-start(s8[6291456]{0:T(1024)(128)(4,1)} %bitcast.14), calls=%async_computation.5 | async-start | bytes 8388608
  20.5 77.1 %slice-start.1 = ((s8[12582912]{0:T(1024)(128)(4,1)}), s8[4194304]{0:T(1024)(128)(4,1)S(1)}, s32[]{:S(2)}) async-start(s8[12582912]{0:T(1024)(128)(4,1)} %bitcast.11), calls=%async_computation.3 | async-start | bytes 8388608
  20.5 5.5 %collective-permute-start.7 = (f32[1024,256]{1,0:T(8,128)S(1)}, f32[1024,256]{1,0:T(8,128)S(1)}, u32[]{:S(2)}, u32[]{:S(2)}) collective-permute-start(f32[1024,256]{1,0:T(8,128)S(1)} %shard_map.131), channel_id=1, source_target_pairs={{0,1},{1,0},{2,3},{3,2},{4,5},{5,4},{6,7},{7,6},{8,9},{9,8},{10,11... | collective-permute-start | bytes 3145736 | tf_op jit(solution)/shard_map/ppermute | solution.py:507
  26.0 29.4 %copy-start = (bf16[16,4096]{1,0:T(8,128)(2,1)S(1)}, bf16[16,4096]{1,0:T(8,128)(2,1)}, u32[]{:S(2)}) copy-start(bf16[16,4096]{1,0:T(8,128)(2,1)} %refs_4_.1) | copy-start | bytes 393220
  26.0 29.4 %copy-start.1 = (f32[4096]{0:T(1024)S(1)}, f32[4096]{0:T(1024)}, u32[]{:S(2)}) copy-start(f32[4096]{0:T(1024)} %param.20) | copy-start | bytes 49156
  26.0 71.5 %slice-start.2 = ((s8[12582912]{0:T(1024)(128)(4,1)}), s8[4194304]{0:T(1024)(128)(4,1)S(1)}, s32[]{:S(2)}) async-start(s8[12582912]{0:T(1024)(128)(4,1)} %bitcast.11), calls=%async_computation.4 | async-start | bytes 8388608
  26.0 71.5 %slice-start.4 = ((s8[6291456]{0:T(1024)(128)(4,1)}), s8[2097152]{0:T(1024)(128)(4,1)S(1)}, s32[]{:S(2)}) async-start(s8[6291456]{0:T(1024)(128)(4,1)} %bitcast.14), calls=%async_computation.6 | async-start | bytes 4194304
  28.0 15.6 %collective-permute-start.10 = (bf16[4,16,4096]{2,1,0:T(8,128)(2,1)S(1)}, bf16[4,16,4096]{2,1,0:T(8,128)(2,1)S(1)}, u32[]{:S(2)}, u32[]{:S(2)}) collective-permute-start(bf16[4,16,4096]{2,1,0:T(8,128)(2,1)S(1)} %get-tuple-element.52), channel_id=1, source_target_pairs={{0,24},{1,97},{2,26},{3,99},{4,28},{5,101},{6,30},{7,103},{8,0},{9... | collective-permute-start | bytes 1572872 | tf_op jit(solution)/shard_map/ppermute | solution.py:511
  31.8 15.2 %collective-permute-start.8 = (bf16[4,16,4096]{2,1,0:T(8,128)(2,1)S(1)}, bf16[4,16,4096]{2,1,0:T(8,128)(2,1)S(1)}, u32[]{:S(2)}, u32[]{:S(2)}) collective-permute-start(bf16[4,16,4096]{2,1,0:T(8,128)(2,1)S(1)} %get-tuple-element.50), channel_id=1, source_target_pairs={{0,8},{1,33},{2,10},{3,35},{4,12},{5,37},{6,14},{7,39},{8,16},{9,4... | collective-permute-start | bytes 1572872 | tf_op jit(solution)/shard_map/ppermute | solution.py:511
  31.8 15.2 %collective-permute-start.9 = (bf16[4,16,4096]{2,1,0:T(8,128)(2,1)S(1)}, bf16[4,16,4096]{2,1,0:T(8,128)(2,1)S(1)}, u32[]{:S(2)}, u32[]{:S(2)}) collective-permute-start(bf16[4,16,4096]{2,1,0:T(8,128)(2,1)S(1)} %get-tuple-element.51), channel_id=1, source_target_pairs={{0,16},{1,65},{2,18},{3,67},{4,20},{5,69},{6,22},{7,71},{8,24},{9,... | collective-permute-start | bytes 1572872 | tf_op jit(solution)/shard_map/ppermute | solution.py:511
  47.9 5.1 %collective-permute-start.11 = (bf16[16,4096]{1,0:T(8,128)(2,1)S(1)}, bf16[16,4096]{1,0:T(8,128)(2,1)S(1)}, u32[]{:S(2)}, u32[]{:S(2)}) collective-permute-start(bf16[16,4096]{1,0:T(8,128)(2,1)S(1)} %get-tuple-element.54), channel_id=1, source_target_pairs={{0,32},{1,9},{2,34},{3,11},{4,36},{5,13},{6,38},{7,15},{8,40},{9,1... | collective-permute-start | bytes 393224 | tf_op jit(solution)/shard_map/ppermute | solution.py:511
  49.0 6.4 %collective-permute-start.12 = (bf16[16,4096]{1,0:T(8,128)(2,1)S(1)}, bf16[16,4096]{1,0:T(8,128)(2,1)S(1)}, u32[]{:S(2)}, u32[]{:S(2)}) collective-permute-start(bf16[16,4096]{1,0:T(8,128)(2,1)S(1)} %get-tuple-element.55), channel_id=1, source_target_pairs={{0,64},{1,17},{2,66},{3,19},{4,68},{5,21},{6,70},{7,23},{8,72},{9,... | collective-permute-start | bytes 393224 | tf_op jit(solution)/shard_map/ppermute | solution.py:511
  51.6 3.8 %collective-permute-start.13 = (bf16[16,4096]{1,0:T(8,128)(2,1)S(1)}, bf16[16,4096]{1,0:T(8,128)(2,1)S(1)}, u32[]{:S(2)}, u32[]{:S(2)}) collective-permute-start(bf16[16,4096]{1,0:T(8,128)(2,1)S(1)} %get-tuple-element.56), channel_id=1, source_target_pairs={{0,96},{1,25},{2,98},{3,27},{4,100},{5,29},{6,102},{7,31},{8,104},... | collective-permute-start | bytes 393224 | tf_op jit(solution)/shard_map/ppermute | solution.py:511
where the time goes:
time: 140 us
  blocking collectives  75.5 us (54%)
  starting transfers between devices  22.6 us (16%)
  Pallas kernels  22.5 us (16%)
  waiting for transfers between devices  18.3 us (13%)
    all_to_all x2, blocking collectives, per_device(): lax.all_to_all(lines, everyone, split_axis=0, concat_axis=0, tiled=True)  75.5 us
    ppermute x6, waiting for transfers between devices, per_device(): lax.ppermute(parts[k], everyone, around(level, k))  16.6 us
    ppermute x6, starting transfers between devices, per_device(): lax.ppermute(parts[k], everyone, around(level, k))  9.89 us
    pallas_call x1, Pallas kernels, experts(): pl.pallas_call(expert_kernel, in_specs=[VMEM(), VMEM(), HBM()], out_specs...  6.85 us
    ppermute x1, starting transfers between devices, per_device(): parts = project(place, mine, swap(far), weight)  3.23 us
  transfers between devices with their start and end apart: 14, of which 7 were waited for; matrix products, arithmetic and copies ran while one was open for 0% of the time, Pallas kernels for 7%

commit v1 on v0

--- a/solution.py
+++ b/solution.py
@@ -53,8 +53,8 @@
     return [(i, (i + step) % 4) for i in range(4)]
 
 
-def prep_kernel(place_ref, cache_ref, new_ref, gain_ref, first, second, cache, new, gain, sems):
-    head = place_ref[1]
+def prep_kernel(cache_ref, new_ref, gain_ref, first, second, cache, new, gain, sems):
+    head = lax.axis_index("z")
     copies = (
         pltpu.make_async_copy(gain_ref, gain, sems.at[0]),
         pltpu.make_async_copy(cache_ref.at[head], cache, sems.at[1]),
@@ -76,10 +76,10 @@
         out_ref[pl.ds(there, rows), HD:] = held[:, HD:]
 
 
-def prep(place, cache, new_kv, k_gain):
+def prep(cache, new_kv, k_gain):
     return pl.pallas_call(
         prep_kernel,
-        in_specs=[SMEM(), HBM(), HBM(), HBM()],
+        in_specs=[HBM()] * 3,
         out_specs=[VMEM()] * 2,
         out_shape=[jax.ShapeDtypeStruct((PART, 2 * HD), BF16)] * 2,
         scratch_shapes=[
@@ -89,7 +89,7 @@
             pltpu.SemaphoreType.DMA((3,)),
         ],
         compiler_params=params(8),
-    )(place, cache, new_kv, k_gain)
+    )(cache, new_kv, k_gain)
 
 
 def join(first, second, whole):
@@ -139,39 +139,35 @@
 STATE = jax.ShapeDtypeStruct((2, QHEADS * QROWS, HD), F32)
 
 
-def near_kernel(place_ref, qn, first, second, weight_ref, acc, total, weight, shard, sem):
-    copy = pltpu.make_async_copy(weight_ref, weight, sem)
-    copy.start()
+def near_kernel(who, place_ref, qn, first, second, acc, total, shard):
     join(first, second, shard)
     acc[...] = jnp.zeros_like(acc)
     total[...] = jnp.zeros_like(total)
-
-    @pl.loop(0, 2)
-    def _(who):
-        add_shard(place_ref, who, 0, shard, qn.at[who], acc.at[who], total.at[who])
-
-    key = lax.broadcasted_iota(jnp.int32, (QHEADS * QROWS, QROWS), 1)
-    query = lax.broadcasted_iota(jnp.int32, (QHEADS * QROWS, QROWS), 0)
-    mask = key <= lax.rem(query, QROWS)
-    add_block(shard, CACHE_ROWS, QROWS, qn.at[0], acc.at[0], total.at[0], mask)
-    copy.wait()
-
-
-def attend_near(place, qn, first, second, weight):
-    return pl.pallas_call(
-        near_kernel,
-        in_specs=[SMEM()] + [VMEM()] * 3 + [HBM()],
-        out_specs=[VMEM()] * 3,
-        out_shape=[STATE, STATE, jax.ShapeDtypeStruct(weight.shape, BF16)],
-        scratch_shapes=[pltpu.VMEM((SHARD, 2 * HD), BF16), pltpu.SemaphoreType.DMA],
-        compiler_params=params(20),
-    )(place, qn, first, second, weight)
-
-
-def middle_kernel(place_ref, qn, acc_ref, total_ref, *refs):
-    parts, (acc, total, shards) = refs[:4], refs[4:]
-    acc[...] = acc_ref[...]
-    total[...] = total_ref[...]
+    add_shard(place_ref, who, 0, shard, qn.at[who], acc, total)
+    if who == 0:
+        key = lax.broadcasted_iota(jnp.int32, (QHEADS * QROWS, QROWS), 1)
+        query = lax.broadcasted_iota(jnp.int32, (QHEADS * QROWS, QROWS), 0)
+        mask = key <= lax.rem(query, QROWS)
+        add_block(shard, CACHE_ROWS, QROWS, qn.at[0], acc, total, mask)
+
+
+def attend_near(who, place, qn, first, second):
+    return pl.pallas_call(
+        functools.partial(near_kernel, who),
+        in_specs=[SMEM()] + [VMEM()] * 3,
+        out_specs=[VMEM()] * 2,
+        out_shape=[jax.ShapeDtypeStruct((QHEADS * QROWS, HD), F32)] * 2,
+        scratch_shapes=[pltpu.VMEM((SHARD, 2 * HD), BF16)],
+        compiler_params=params(16),
+    )(place, qn, first, second)
+
+
+def middle_kernel(place_ref, qn, own_acc, own_total, other_acc, other_total, *refs):
+    parts, (weight_ref, acc, total, weight, shards, sem) = refs[:4], refs[4:]
+    copy = pltpu.make_async_copy(weight_ref, weight, sem)
+    copy.start()
+    acc[0], total[0] = own_acc[...], own_total[...]
+    acc[1], total[1] = other_acc[...], other_total[...]
     join(parts[0], parts[1], shards.at[0])
     join(parts[2], parts[3], shards.at[1])
 
@@ -183,16 +179,18 @@
             place_ref, who, distance, shards.at[side], qn.at[who], acc.at[who], total.at[who]
         )
 
-
-def attend_middle(place, qn, acc, total, parts):
+    copy.wait()
+
+
+def attend_middle(place, qn, own, other, parts, weight):
     return pl.pallas_call(
         middle_kernel,
-        in_specs=[SMEM()] + [VMEM()] * 7,
-        out_specs=[VMEM()] * 2,
-        out_shape=[STATE] * 2,
-        scratch_shapes=[pltpu.VMEM((2, SHARD, 2 * HD), BF16)],
-        compiler_params=params(16),
-    )(place, qn, acc, total, *parts)
+        in_specs=[SMEM()] + [VMEM()] * 9 + [HBM()],
+        out_specs=[VMEM()] * 3,
+        out_shape=[STATE, STATE, jax.ShapeDtypeStruct(weight.shape, BF16)],
+        scratch_shapes=[pltpu.VMEM((2, SHARD, 2 * HD), BF16), pltpu.SemaphoreType.DMA],
+        compiler_params=params(20),
+    )(place, qn, *own, *other, *parts, weight)
 
 
 def far_kernel(who, place_ref, qn, acc_ref, total_ref, first, second, out_ref, acc, total, shard):
@@ -200,8 +198,8 @@
     total[...] = total_ref[who]
     join(first, second, shard)
     add_shard(place_ref, who, 2, shard, qn.at[who], acc, total)
-    out_ref[:, :HD] = acc[...]
-    out_ref[:, HD:] = total[...]
+    out_ref[:, :HD] = acc[...].astype(out_ref.dtype)
+    out_ref[:, HD:] = total[...].astype(out_ref.dtype)
 
 
 def attend_far(who, place, qn, acc, total, first, second):
@@ -209,7 +207,7 @@
         functools.partial(far_kernel, who),
         in_specs=[SMEM()] + [VMEM()] * 5,
         out_specs=VMEM(),
-        out_shape=jax.ShapeDtypeStruct((QHEADS * QROWS, 2 * HD), F32),
+        out_shape=jax.ShapeDtypeStruct((QHEADS * QROWS, 2 * HD), BF16 if who else F32),
         scratch_shapes=[
             pltpu.VMEM((QHEADS * QROWS, HD), F32),
             pltpu.VMEM((QHEADS * QROWS, HD), F32),
@@ -224,7 +222,7 @@
     z, y, c = place_ref[1], place_ref[2], place_ref[4]
     for h in range(QHEADS):
         at = pl.ds(h * QROWS, QROWS)
-        both = own_ref[at, :] + other_ref[at, :]
+        both = own_ref[at, :] + other_ref[at, :].astype(F32)
         whole = jnp.sum(both[:, HD:], axis=1, keepdims=True)
         attn[:, h * HD : (h + 1) * HD] = (both[:, :HD] / whole).astype(BF16)
     for k in range(4):
@@ -388,10 +386,8 @@
 
 
 def expert_kernel(
-    lines_ref, up_ref, down_hbm, out_ref, rows, both, active, back, down_ref, sem
+    lines_ref, up_ref, down_ref, out_ref, rows, both, active, back
 ):
-    copy = pltpu.make_async_copy(down_hbm, down_ref, sem)
-    copy.start()
     size = (GROUP_LINES, GROUP_LINES)
     first = lax.broadcasted_iota(jnp.int32, size, 0)
     second = lax.broadcasted_iota(jnp.int32, size, 1)
@@ -415,7 +411,6 @@
         both[:, columns] = jnp.dot(rows[...], up_ref[:, columns], preferred_element_type=F32)
     gate = both[:, :FFE]
     active[...] = (gate * jax.nn.sigmoid(gate) * both[:, FFE:]).astype(BF16)
-    copy.wait()
     for k in range(CHUNKS):
         columns = slice(k * PIECE, (k + 1) * PIECE)
         down = jnp.dot(active[...], down_ref[:, columns], preferred_element_type=F32)
@@ -430,7 +425,7 @@
 def experts(lines, gate_up, down):
     return pl.pallas_call(
         expert_kernel,
-        in_specs=[VMEM(), VMEM(), HBM()],
+        in_specs=[VMEM()] * 3,
         out_specs=VMEM(),
         out_shape=jax.ShapeDtypeStruct((EXPERTS, LINES, PIECE), BF16),
         scratch_shapes=[
@@ -438,10 +433,8 @@
             pltpu.VMEM((EXPERTS * SLOTS, 2 * FFE), F32),
             pltpu.VMEM((EXPERTS * SLOTS, FFE), BF16),
             pltpu.VMEM((8, GROUP_LINES, PIECE), BF16),
-            pltpu.VMEM((FFE, WIDTH), BF16),
-            pltpu.SemaphoreType.DMA,
         ],
-        compiler_params=params(24),
+        compiler_params=params(18),
     )(lines, gate_up, down)
 
 
@@ -487,19 +480,20 @@
     swap = functools.partial(lax.ppermute, axis_name="c", perm=[(0, 1), (1, 0)])
     other = swap(queries)
     left, right = shift(1), shift(3)
-    own = prep(place, held(cache), held(new_kv), held(k_gain.reshape(1, HD)))
+    own = prep(held(cache), held(new_kv), held(k_gain.reshape(1, HD)))
     first_left, second_right = lax.ppermute(own[0], "x", left), lax.ppermute(own[1], "x", right)
     second_left, first_right = lax.ppermute(own[1], "x", left), lax.ppermute(own[0], "x", right)
     placing, mixing, qn = route(
         held(expert_ids.T), held(combine_weight.T), held(queries), held(q_gain.reshape(1, HD)), other
     )
-    first_left, second_right, placing, mixing, qn = lax.optimization_barrier(
-        (first_left, second_right, placing, mixing, qn)
+    other = attend_near(1, place, qn, *own)
+    first_left, second_right, placing, mixing, qn, *other = lax.optimization_barrier(
+        (first_left, second_right, placing, mixing, qn, *other)
     )
     first, second = lax.ppermute(first_left, "x", left), lax.ppermute(second_right, "x", right)
-    acc, total, weight = attend_near(place, qn, *own, held(out_weight))
+    mine = attend_near(0, place, qn, *own)
     parts = (first_left, second_left, first_right, second_right)
-    acc, total = attend_middle(place, qn, acc, total, parts)
+    acc, total, weight = attend_middle(place, qn, mine, other, parts, held(out_weight))
     far = attend_far(1, place, qn, acc, total, first, second)
     far, acc, total = lax.optimization_barrier((far, acc, total))
     mine = attend_far(0, place, qn, acc, total, first, second)

time: 140 us -> 137 us (0.979)
  blocking collectives: 75.5 us -> 72.1 us
  waiting for transfers between devices: 18.3 us -> 16.7 us
  Pallas kernels: 22.5 us -> 24 us
    all_to_all x2, blocking collectives: 75.5 us -> 72.1 us  [per_device(): lax.all_to_all(lines, everyone, split_axis=0, concat_axis=0, tiled=True)]
    ppermute x1, waiting for transfers between devices: 1.56 us -> 0.07 us  [per_device(): parts = project(place, mine, swap(far), weight)]
    pallas_call x4 -> x5, Pallas kernels: 13.7 us -> 13.9 us  [the longest x1 6.26 us: experts(): pl.pallas_call(expert_kernel, in_specs=[VMEM()] * 3, out_specs=VMEM(), ou...]
  transfers between devices with their start and end apart: 14 -> 14, of which waited for: 7 -> 6; matrix products, arithmetic and copies ran while one was open for 0% -> 0% of each run, Pallas kernels for 7% -> 8%
where the time goes in v1:
time: 137 us; the launch traced here: 136 us
  blocking collectives  72.1 us (53%)
  Pallas kernels  24 us (18%)
  starting transfers between devices  22.7 us (17%)
  waiting for transfers between devices  16.7 us (12%)
    all_to_all x2, blocking collectives, per_device(): lax.all_to_all(lines, everyone, split_axis=0, concat_axis=0, tiled=True)  72.1 us
    ppermute x6, waiting for transfers between devices, per_device(): lax.ppermute(parts[k], everyone, around(level, k))  16.6 us
    ppermute x6, starting transfers between devices, per_device(): lax.ppermute(parts[k], everyone, around(level, k))  10.2 us
    pallas_call x1, Pallas kernels, experts(): pl.pallas_call(expert_kernel, in_specs=[VMEM()] * 3, out_specs=VMEM(), ou...  6.26 us
    pallas_call x2, Pallas kernels, attend_near(): pl.pallas_call(functools.partial(near_kernel, who), in_specs=[SMEM()] + [...  3.46 us
    pallas_call x1, Pallas kernels, attend_middle(): pl.pallas_call(middle_kernel, in_specs=[SMEM()] + [VMEM()] * 9 + [HBM()],...  3.01 us
    ppermute x1, starting transfers between devices, per_device(): parts = project(place, mine, swap(far), weight)  2.9 us
    pallas_call x2, Pallas kernels, attend_far(): pl.pallas_call(functools.partial(far_kernel, who), in_specs=[SMEM()] + [V...  2.87 us
  transfers between devices with their start and end apart: 14, of which 6 were waited for; matrix products, arithmetic and copies ran while one was open for 0% of the time, Pallas kernels for 8%

profile of v1, /device:TPU:1, one launch (start us, length us, event | category | flops | bytes accessed | tf_op | source)
XLA Modules:
  0.0 136.5 jit_solution(7719082890794462415)
XLA Ops:
  0.0 1.4 %collective-permute-start.2 = (bf16[256,512]{1,0:T(8,128)(2,1)}, bf16[256,512]{1,0:T(8,128)(2,1)S(1)}, u32[]{:S(2)}, u32[]{:S(2)}) collective-permute-start(bf16[256,512]{1,0:T(8,128)(2,1)} %q_ref.1), channel_id=1, source_target_pairs={{0,1},{1,0},{2,3},{3,2},{4,5},{5,4},{6,7},{7,6},{8,9},{9,8},{10,11... | collective-permute-start | bytes 786440 | tf_op jit(solution)/shard_map/ppermute | solution.py:481
  1.4 1.2 shard_map.127
  2.6 1.4 collective-permute-start
  4.0 1.4 %collective-permute-start.1 = (bf16[384,256]{1,0:T(8,128)(2,1)S(1)}, bf16[384,256]{1,0:T(8,128)(2,1)S(1)}, u32[]{:S(2)}, u32[]{:S(2)}) collective-permute-start(bf16[384,256]{1,0:T(8,128)(2,1)S(1)} %get-tuple-element.38.second), channel_id=1, source_target_pairs={{0,6},{2,0},{4,2},{6,4},{1,7},{3,1},{5,3},{7,5},{8,14},{10,8},{12,... | collective-permute-start | bytes 589832 | tf_op jit(solution)/shard_map/ppermute | solution.py:484
  5.5 2.6 %collective-permute-start.4 = (bf16[384,256]{1,0:T(8,128)(2,1)S(1)}, bf16[384,256]{1,0:T(8,128)(2,1)S(1)}, u32[]{:S(2)}, u32[]{:S(2)}) collective-permute-start(bf16[384,256]{1,0:T(8,128)(2,1)S(1)} %get-tuple-element.37.first), channel_id=1, source_target_pairs={{0,6},{2,0},{4,2},{6,4},{1,7},{3,1},{5,3},{7,5},{8,14},{10,8},{12,... | collective-permute-start | bytes 589832 | tf_op jit(solution)/shard_map/ppermute | solution.py:485
  8.8 2.2 %shard_map.128 = (bf16[2048,128]{1,0:T(8,128)(2,1)S(1)}, bf16[2048,128]{1,0:T(8,128)(2,1)S(1)}, bf16[2,1024,128]{2,1,0:T(8,128)(2,1)S(1)}) custom-call(s32[8,16]{1,0:T(8,128)} %bitcast.18, bf16[8,16]{1,0:T(8,128)(2,1)} %bitcast.19, bf16[256,512]{1,0:T(8,128)(2,1)} %q_ref.1, f32[1,128]{1,0:T(1,128)} %bitcast.21, ...), custom_call_target="tpu_custom_call" | custom-call | tf_op jit(solution)/shard_map/pallas_call | solution.py:336
  11.0 1.4 %shard_map.129 = (f32[1024,128]{1,0:T(8,128)S(1)}, f32[1024,128]{1,0:T(8,128)S(1)}) custom-call(s32[5]{0:T(128)S(1)} %stack.19.place_ref, bf16[2,1024,128]{2,1,0:T(8,128)(2,1)S(1)} %get-tuple-element.44.qn, bf16[384,256]{1,0:T(8,128)(2,1)S(1)} %get-tuple-element.37.first, bf16[384,256]{1,0:T(8,128)(2,1)S(1)} %get-tuple-element.38.second), custom_call_target="tpu_custom_call" | custom-call | tf_op jit(solution)/shard_map/pallas_call | solution.py:155
  12.5 2.7 %collective-permute-start.6 = (bf16[384,256]{1,0:T(8,128)(2,1)S(1)}, bf16[384,256]{1,0:T(8,128)(2,1)S(1)}, u32[]{:S(2)}, u32[]{:S(2)}) collective-permute-start(bf16[384,256]{1,0:T(8,128)(2,1)S(1)} %collective-permute-done.1.refs_3_), channel_id=1, source_target_pairs={{0,6},{2,0},{4,2},{6,4},{1,7},{3,1},{5,3},{7,5},{8,14},{10,8},{12,... | collective-permute-start | bytes 589832 | tf_op jit(solution)/shard_map/ppermute | solution.py:493
  15.2 2.1 %shard_map.130 = (f32[1024,128]{1,0:T(8,128)S(1)}, f32[1024,128]{1,0:T(8,128)S(1)}) custom-call(s32[5]{0:T(128)S(1)} %stack.19.place_ref, bf16[2,1024,128]{2,1,0:T(8,128)(2,1)S(1)} %get-tuple-element.44.qn, bf16[384,256]{1,0:T(8,128)(2,1)S(1)} %get-tuple-element.37.first, bf16[384,256]{1,0:T(8,128)(2,1)S(1)} %get-tuple-element.38.second), custom_call_target="tpu_custom_call" | custom-call | tf_op jit(solution)/shard_map/pallas_call | solution.py:155
  17.3 3.0 %shard_map.131 = (f32[2,1024,128]{2,1,0:T(8,128)S(1)}, f32[2,1024,128]{2,1,0:T(8,128)S(1)}, bf16[512,4096]{1,0:T(8,128)(2,1)S(1)}) custom-call(s32[5]{0:T(128)S(1)} %stack.19.place_ref, bf16[2,1024,128]{2,1,0:T(8,128)(2,1)S(1)} %get-tuple-element.44.qn, f32[1024,128]{1,0:T(8,128)S(1)} %get-tuple-element.45.own_acc, ...), custom_call_target="tpu_custom_call" | custom-call | tf_op jit(solution)/shard_map/pallas_call | solution.py:186
  20.4 1.4 %shard_map.132 = bf16[1024,256]{1,0:T(8,128)(2,1)S(1)} custom-call(s32[5]{0:T(128)S(1)} %stack.19.place_ref, bf16[2,1024,128]{2,1,0:T(8,128)(2,1)S(1)} %get-tuple-element.44.qn, f32[2,1024,128]{2,1,0:T(8,128)S(1)} %get-tuple-element.53.acc_ref, f32[2,1024,128]{2,1,0:T(8,128)S(1)} %get-tuple-element.54.total_ref, ...), custom_call_target="tpu_custom_call" | custom-call | tf_op jit(solution)/shard_map/pallas_call | solution.py:206
  21.8 2.9 %collective-permute-start.7 = (bf16[1024,256]{1,0:T(8,128)(2,1)S(1)}, bf16[1024,256]{1,0:T(8,128)(2,1)S(1)}, u32[]{:S(2)}, u32[]{:S(2)}) collective-permute-start(bf16[1024,256]{1,0:T(8,128)(2,1)S(1)} %shard_map.132), channel_id=1, source_target_pairs={{0,1},{1,0},{2,3},{3,2},{4,5},{5,4},{6,7},{7,6},{8,9},{9,8},{10,11... | collective-permute-start | bytes 1572872 | tf_op jit(solution)/shard_map/ppermute | solution.py:501
  24.7 1.4 %shard_map.133.own_ref = f32[1024,256]{1,0:T(8,128)S(1)} custom-call(s32[5]{0:T(128)S(1)} %stack.19.place_ref, bf16[2,1024,128]{2,1,0:T(8,128)(2,1)S(1)} %get-tuple-element.44.qn, f32[2,1024,128]{2,1,0:T(8,128)S(1)} %get-tuple-element.53.acc_ref, f32[2,1024,128]{2,1,0:T(8,128)S(1)} %get-tuple-element.54.total_ref, ...), custom_call_target="tpu_custom_call" | custom-call | tf_op jit(solution)/shard_map/pallas_call | solution.py:206
  26.3 2.0 %shard_map.134 = (bf16[4,16,4096]{2,1,0:T(8,128)(2,1)S(1)}, bf16[4,16,4096]{2,1,0:T(8,128)(2,1)S(1)}, bf16[4,16,4096]{2,1,0:T(8,128)(2,1)S(1)}, bf16[4,16,4096]{2,1,0:T(8,128)(2,1)S(1)}) custom-call(s32[5]{0:T(128)S(1)} %stack.19.place_ref, f32[1024,256]{1,0:T(8,128)S(1)} %shard_map.133.own_ref, bf16[1024,256]{1,0:T(8,128)(2,1)S(1)} %collective-permute-done.7.other_ref, ...), custom_call_target="tpu_custom_call" | custom-call | tf_op jit(solution)/shard_map/pallas_call | solution.py:244
  28.3 3.9 %collective-permute-start.10 = (bf16[4,16,4096]{2,1,0:T(8,128)(2,1)S(1)}, bf16[4,16,4096]{2,1,0:T(8,128)(2,1)S(1)}, u32[]{:S(2)}, u32[]{:S(2)}) collective-permute-start(bf16[4,16,4096]{2,1,0:T(8,128)(2,1)S(1)} %get-tuple-element.60), channel_id=1, source_target_pairs={{0,24},{1,97},{2,26},{3,99},{4,28},{5,101},{6,30},{7,103},{8,0},{9... | collective-permute-start | bytes 1572872 | tf_op jit(solution)/shard_map/ppermute | solution.py:505
  32.2 1.3 collective-permute-start.9
  33.5 10.4 %collective-permute-done.10.refs_3_ = bf16[4,16,4096]{2,1,0:T(8,128)(2,1)S(1)} collective-permute-done((bf16[4,16,4096]{2,1,0:T(8,128)(2,1)S(1)}, bf16[4,16,4096]{2,1,0:T(8,128)(2,1)S(1)}, u32[]{:S(2)}, u32[]{:S(2)}) %collective-permute-start.10) | collective-permute-done | bytes 524320 | tf_op jit(solution)/shard_map/ppermute | solution.py:505
  43.9 3.4 %collective-permute-done.8.refs_1_ = bf16[4,16,4096]{2,1,0:T(8,128)(2,1)S(1)} collective-permute-done((bf16[4,16,4096]{2,1,0:T(8,128)(2,1)S(1)}, bf16[4,16,4096]{2,1,0:T(8,128)(2,1)S(1)}, u32[]{:S(2)}, u32[]{:S(2)}) %collective-permute-start.8) | collective-permute-done | bytes 524320 | tf_op jit(solution)/shard_map/ppermute | solution.py:505
  48.3 1.3 collective-permute-start.11
  49.6 2.6 %collective-permute-start.12 = (bf16[16,4096]{1,0:T(8,128)(2,1)S(1)}, bf16[16,4096]{1,0:T(8,128)(2,1)S(1)}, u32[]{:S(2)}, u32[]{:S(2)}) collective-permute-start(bf16[16,4096]{1,0:T(8,128)(2,1)S(1)} %get-tuple-element.63), channel_id=1, source_target_pairs={{0,64},{1,17},{2,66},{3,19},{4,68},{5,21},{6,70},{7,23},{8,72},{9,... | collective-permute-start | bytes 393224 | tf_op jit(solution)/shard_map/ppermute | solution.py:505
  53.6 2.3 %collective-permute-done.12.refs_2_ = bf16[16,4096]{1,0:T(8,128)(2,1)S(1)} collective-permute-done((bf16[16,4096]{1,0:T(8,128)(2,1)S(1)}, bf16[16,4096]{1,0:T(8,128)(2,1)S(1)}, u32[]{:S(2)}, u32[]{:S(2)}) %collective-permute-start.12) | collective-permute-done | bytes 131104 | tf_op jit(solution)/shard_map/ppermute | solution.py:505
  56.9 37.7 %all_to_all.10.lines_ref = bf16[128,16,512]{2,1,0:T(8,128)(2,1)S(1)} all-to-all(bf16[128,16,512]{2,1,0:T(8,128)(2,1)S(1)} %get-tuple-element.66), channel_id=1, replica_groups=mesh['z'=4,'y'=4,'x'=4,'c'=2] {'z','y','x','c'}, dimensions={0} | all-to-all | bytes 4194304 | tf_op jit(solution)/shard_map/all_to_all | solution.py:508
  94.7 6.3 %shard_map.137 = bf16[128,16,512]{2,1,0:T(8,128)(2,1)S(1)} custom-call(bf16[128,16,512]{2,1,0:T(8,128)(2,1)S(1)} %all_to_all.10.lines_ref, bf16[4096,1536]{1,0:T(8,128)(2,1)S(1)} %bitcast.13, bf16[768,4096]{1,0:T(8,128)(2,1)S(1)} %bitcast.16), custom_call_target="tpu_custom_call" | custom-call | tf_op jit(solution)/shard_map/pallas_call | solution.py:426
  100.9 34.4 %all_to_all.11.lines_ref = bf16[128,16,512]{2,1,0:T(8,128)(2,1)S(1)} all-to-all(bf16[128,16,512]{2,1,0:T(8,128)(2,1)S(1)} %shard_map.137), channel_id=1, replica_groups=mesh['z'=4,'y'=4,'x'=4,'c'=2] {'z','y','x','c'}, dimensions={0} | all-to-all | bytes 4194304 | tf_op jit(solution)/shard_map/all_to_all | solution.py:510
  (35 shorter events, 4.8 us)
Async XLA Ops:
  0.0 8.8 %collective-permute-start.2 = (bf16[256,512]{1,0:T(8,128)(2,1)}, bf16[256,512]{1,0:T(8,128)(2,1)S(1)}, u32[]{:S(2)}, u32[]{:S(2)}) collective-permute-start(bf16[256,512]{1,0:T(8,128)(2,1)} %q_ref.1), channel_id=1, source_target_pairs={{0,1},{1,0},{2,3},{3,2},{4,5},{5,4},{6,7},{7,6},{8,9},{9,8},{10,11... | collective-permute-start | bytes 786440 | tf_op jit(solution)/shard_map/ppermute | solution.py:481
  2.6 9.8 %collective-permute-start = (bf16[384,256]{1,0:T(8,128)(2,1)S(1)}, bf16[384,256]{1,0:T(8,128)(2,1)S(1)}, u32[]{:S(2)}, u32[]{:S(2)}) collective-permute-start(bf16[384,256]{1,0:T(8,128)(2,1)S(1)} %get-tuple-element.37.first), channel_id=1, source_target_pairs={{0,2},{2,4},{4,6},{6,0},{1,3},{3,5},{5,7},{7,1},{8,10},{10,12},{12... | collective-permute-start | bytes 589832 | tf_op jit(solution)/shard_map/ppermute | solution.py:484
  4.0 8.4 %collective-permute-start.1 = (bf16[384,256]{1,0:T(8,128)(2,1)S(1)}, bf16[384,256]{1,0:T(8,128)(2,1)S(1)}, u32[]{:S(2)}, u32[]{:S(2)}) collective-permute-start(bf16[384,256]{1,0:T(8,128)(2,1)S(1)} %get-tuple-element.38.second), channel_id=1, source_target_pairs={{0,6},{2,0},{4,2},{6,4},{1,7},{3,1},{5,3},{7,5},{8,14},{10,8},{12,... | collective-permute-start | bytes 589832 | tf_op jit(solution)/shard_map/ppermute | solution.py:484
  5.4 11.9 %collective-permute-start.3 = (bf16[384,256]{1,0:T(8,128)(2,1)S(1)}, bf16[384,256]{1,0:T(8,128)(2,1)S(1)}, u32[]{:S(2)}, u32[]{:S(2)}) collective-permute-start(bf16[384,256]{1,0:T(8,128)(2,1)S(1)} %get-tuple-element.38.second), channel_id=1, source_target_pairs={{0,2},{2,4},{4,6},{6,0},{1,3},{3,5},{5,7},{7,1},{8,10},{10,12},{12... | collective-permute-start | bytes 589832 | tf_op jit(solution)/shard_map/ppermute | solution.py:485
  5.5 11.8 %collective-permute-start.4 = (bf16[384,256]{1,0:T(8,128)(2,1)S(1)}, bf16[384,256]{1,0:T(8,128)(2,1)S(1)}, u32[]{:S(2)}, u32[]{:S(2)}) collective-permute-start(bf16[384,256]{1,0:T(8,128)(2,1)S(1)} %get-tuple-element.37.first), channel_id=1, source_target_pairs={{0,6},{2,0},{4,2},{6,4},{1,7},{3,1},{5,3},{7,5},{8,14},{10,8},{12,... | collective-permute-start | bytes 589832 | tf_op jit(solution)/shard_map/ppermute | solution.py:485
  12.4 7.9 %collective-permute-start.5 = (bf16[384,256]{1,0:T(8,128)(2,1)S(1)}, bf16[384,256]{1,0:T(8,128)(2,1)S(1)}, u32[]{:S(2)}, u32[]{:S(2)}) collective-permute-start(bf16[384,256]{1,0:T(8,128)(2,1)S(1)} %collective-permute-done.refs_0_), channel_id=1, source_target_pairs={{0,2},{2,4},{4,6},{6,0},{1,3},{3,5},{5,7},{7,1},{8,10},{10,12},{12... | collective-permute-start | bytes 589832 | tf_op jit(solution)/shard_map/ppermute | solution.py:493
  12.5 7.8 %collective-permute-start.6 = (bf16[384,256]{1,0:T(8,128)(2,1)S(1)}, bf16[384,256]{1,0:T(8,128)(2,1)S(1)}, u32[]{:S(2)}, u32[]{:S(2)}) collective-permute-start(bf16[384,256]{1,0:T(8,128)(2,1)S(1)} %collective-permute-done.1.refs_3_), channel_id=1, source_target_pairs={{0,6},{2,0},{4,2},{6,4},{1,7},{3,1},{5,3},{7,5},{8,14},{10,8},{12,... | collective-permute-start | bytes 589832 | tf_op jit(solution)/shard_map/ppermute | solution.py:493
  17.3 77.3 %slice-start = ((s8[12582912]{0:T(1024)(128)(4,1)}), s8[4194304]{0:T(1024)(128)(4,1)S(1)}, s32[]{:S(2)}) async-start(s8[12582912]{0:T(1024)(128)(4,1)} %bitcast.11), calls=%async_computation.2 | async-start | bytes 8388608
  20.4 74.3 %slice-start.1 = ((s8[12582912]{0:T(1024)(128)(4,1)}), s8[4194304]{0:T(1024)(128)(4,1)S(1)}, s32[]{:S(2)}) async-start(s8[12582912]{0:T(1024)(128)(4,1)} %bitcast.11), calls=%async_computation.3 | async-start | bytes 8388608
  21.8 4.4 %collective-permute-start.7 = (bf16[1024,256]{1,0:T(8,128)(2,1)S(1)}, bf16[1024,256]{1,0:T(8,128)(2,1)S(1)}, u32[]{:S(2)}, u32[]{:S(2)}) collective-permute-start(bf16[1024,256]{1,0:T(8,128)(2,1)S(1)} %shard_map.132), channel_id=1, source_target_pairs={{0,1},{1,0},{2,3},{3,2},{4,5},{5,4},{6,7},{7,6},{8,9},{9,8},{10,11... | collective-permute-start | bytes 1572872 | tf_op jit(solution)/shard_map/ppermute | solution.py:501
  24.7 69.9 %slice-start.3 = ((s8[6291456]{0:T(1024)(128)(4,1)}), s8[4194304]{0:T(1024)(128)(4,1)S(1)}, s32[]{:S(2)}) async-start(s8[6291456]{0:T(1024)(128)(4,1)} %bitcast.14), calls=%async_computation.5 | async-start | bytes 8388608
  26.2 29.9 %copy-start = (bf16[16,4096]{1,0:T(8,128)(2,1)S(1)}, bf16[16,4096]{1,0:T(8,128)(2,1)}, u32[]{:S(2)}) copy-start(bf16[16,4096]{1,0:T(8,128)(2,1)} %refs_4_.3) | copy-start | bytes 393220
  26.2 29.8 %copy-start.1 = (f32[4096]{0:T(1024)S(1)}, f32[4096]{0:T(1024)}, u32[]{:S(2)}) copy-start(f32[4096]{0:T(1024)} %param.20) | copy-start | bytes 49156
  26.3 68.4 %slice-start.2 = ((s8[12582912]{0:T(1024)(128)(4,1)}), s8[4194304]{0:T(1024)(128)(4,1)S(1)}, s32[]{:S(2)}) async-start(s8[12582912]{0:T(1024)(128)(4,1)} %bitcast.11), calls=%async_computation.4 | async-start | bytes 8388608
  26.3 68.4 %slice-start.4 = ((s8[6291456]{0:T(1024)(128)(4,1)}), s8[2097152]{0:T(1024)(128)(4,1)S(1)}, s32[]{:S(2)}) async-start(s8[6291456]{0:T(1024)(128)(4,1)} %bitcast.14), calls=%async_computation.6 | async-start | bytes 4194304
  28.3 15.7 %collective-permute-start.10 = (bf16[4,16,4096]{2,1,0:T(8,128)(2,1)S(1)}, bf16[4,16,4096]{2,1,0:T(8,128)(2,1)S(1)}, u32[]{:S(2)}, u32[]{:S(2)}) collective-permute-start(bf16[4,16,4096]{2,1,0:T(8,128)(2,1)S(1)} %get-tuple-element.60), channel_id=1, source_target_pairs={{0,24},{1,97},{2,26},{3,99},{4,28},{5,101},{6,30},{7,103},{8,0},{9... | collective-permute-start | bytes 1572872 | tf_op jit(solution)/shard_map/ppermute | solution.py:505
  32.2 15.2 %collective-permute-start.8 = (bf16[4,16,4096]{2,1,0:T(8,128)(2,1)S(1)}, bf16[4,16,4096]{2,1,0:T(8,128)(2,1)S(1)}, u32[]{:S(2)}, u32[]{:S(2)}) collective-permute-start(bf16[4,16,4096]{2,1,0:T(8,128)(2,1)S(1)} %get-tuple-element.58), channel_id=1, source_target_pairs={{0,8},{1,33},{2,10},{3,35},{4,12},{5,37},{6,14},{7,39},{8,16},{9,4... | collective-permute-start | bytes 1572872 | tf_op jit(solution)/shard_map/ppermute | solution.py:505
  32.2 15.2 %collective-permute-start.9 = (bf16[4,16,4096]{2,1,0:T(8,128)(2,1)S(1)}, bf16[4,16,4096]{2,1,0:T(8,128)(2,1)S(1)}, u32[]{:S(2)}, u32[]{:S(2)}) collective-permute-start(bf16[4,16,4096]{2,1,0:T(8,128)(2,1)S(1)} %get-tuple-element.59), channel_id=1, source_target_pairs={{0,16},{1,65},{2,18},{3,67},{4,20},{5,69},{6,22},{7,71},{8,24},{9,... | collective-permute-start | bytes 1572872 | tf_op jit(solution)/shard_map/ppermute | solution.py:505
  48.3 5.3 %collective-permute-start.11 = (bf16[16,4096]{1,0:T(8,128)(2,1)S(1)}, bf16[16,4096]{1,0:T(8,128)(2,1)S(1)}, u32[]{:S(2)}, u32[]{:S(2)}) collective-permute-start(bf16[16,4096]{1,0:T(8,128)(2,1)S(1)} %get-tuple-element.62), channel_id=1, source_target_pairs={{0,32},{1,9},{2,34},{3,11},{4,36},{5,13},{6,38},{7,15},{8,40},{9,1... | collective-permute-start | bytes 393224 | tf_op jit(solution)/shard_map/ppermute | solution.py:505
  49.6 6.4 %collective-permute-start.12 = (bf16[16,4096]{1,0:T(8,128)(2,1)S(1)}, bf16[16,4096]{1,0:T(8,128)(2,1)S(1)}, u32[]{:S(2)}, u32[]{:S(2)}) collective-permute-start(bf16[16,4096]{1,0:T(8,128)(2,1)S(1)} %get-tuple-element.63), channel_id=1, source_target_pairs={{0,64},{1,17},{2,66},{3,19},{4,68},{5,21},{6,70},{7,23},{8,72},{9,... | collective-permute-start | bytes 393224 | tf_op jit(solution)/shard_map/ppermute | solution.py:505
  52.2 3.8 %collective-permute-start.13 = (bf16[16,4096]{1,0:T(8,128)(2,1)S(1)}, bf16[16,4096]{1,0:T(8,128)(2,1)S(1)}, u32[]{:S(2)}, u32[]{:S(2)}) collective-permute-start(bf16[16,4096]{1,0:T(8,128)(2,1)S(1)} %get-tuple-element.64), channel_id=1, source_target_pairs={{0,96},{1,25},{2,98},{3,27},{4,100},{5,29},{6,102},{7,31},{8,104},... | collective-permute-start | bytes 393224 | tf_op jit(solution)/shard_map/ppermute | solution.py:505

commit v2 on v1

--- a/solution.py
+++ b/solution.py
@@ -285,16 +285,37 @@
     )(place, *parts)
 
 
-def route_kernel(
-    ids_hbm, weights_hbm, q_ref, gain_ref, other_ref, placing_ref, mixing_ref, qn,
-    ids_ref, weights_ref, queries, gain, sems,
-):
-    pairs = ((gain_ref, gain), (q_ref, queries), (ids_hbm, ids_ref), (weights_hbm, weights_ref))
-    copies = [pltpu.make_async_copy(a, b, sems.at[i]) for i, (a, b) in enumerate(pairs)]
+def query_kernel(q_ref, gain_ref, other_ref, qn, queries, gain, sems):
+    copies = (
+        pltpu.make_async_copy(gain_ref, gain, sems.at[0]),
+        pltpu.make_async_copy(q_ref, queries, sems.at[1]),
+    )
     for copy in copies:
         copy.start()
     for copy in copies:
         copy.wait()
+    for who, ref in enumerate((queries, other_ref)):
+        for h in range(QHEADS):
+            head = ref[:, h * HD : (h + 1) * HD].astype(F32)
+            qn[who, pl.ds(h * QROWS, QROWS), :] = rms_scale(head, gain[...]).astype(BF16)
+
+
+def norm_queries(queries, q_gain, other):
+    return pl.pallas_call(
+        query_kernel,
+        in_specs=[HBM()] * 2 + [VMEM()],
+        out_specs=VMEM(),
+        out_shape=jax.ShapeDtypeStruct((2, QHEADS * QROWS, HD), BF16),
+        scratch_shapes=[
+            pltpu.VMEM((QROWS, QHEADS * HD), BF16),
+            pltpu.VMEM((1, HD), F32),
+            pltpu.SemaphoreType.DMA((2,)),
+        ],
+        compiler_params=params(16),
+    )(queries, q_gain, other)
+
+
+def route_kernel(ids_ref, weights_ref, placing_ref, mixing_ref):
     square = (EXPERTS, EXPERTS)
     expert = lax.broadcasted_iota(jnp.int32, square, 0)
     lane = lax.broadcasted_iota(jnp.int32, square, 1)
@@ -325,29 +346,21 @@
             pick = jnp.where(of_expert & (line % SLOTS == s), 1.0, 0.0).astype(BF16)
             slot = jnp.where(before == s, held, 0.0).astype(BF16)
             table = table + jnp.dot(pick, slot, preferred_element_type=F32)
-        out_ref[...] = jnp.where(same, table, 0.0).astype(BF16)
-    for who, ref in enumerate((queries, other_ref)):
-        for h in range(QHEADS):
-            head = ref[:, h * HD : (h + 1) * HD].astype(F32)
-            qn[who, pl.ds(h * QROWS, QROWS), :] = rms_scale(head, gain[...]).astype(BF16)
-
-
-def route(expert_ids, combine_weight, queries, q_gain, other):
+        table = jnp.where(same, table, 0.0)
+        out_ref[...] = (table if out_ref is placing_ref else table.T).astype(BF16)
+
+
+def route(expert_ids, combine_weight):
     return pl.pallas_call(
         route_kernel,
-        in_specs=[HBM()] * 4 + [VMEM()],
-        out_specs=[VMEM()] * 3,
-        out_shape=[jax.ShapeDtypeStruct((EXPERTS * LINES, EXPERTS), BF16)] * 2
-        + [jax.ShapeDtypeStruct((2, QHEADS * QROWS, HD), BF16)],
-        scratch_shapes=[
-            pltpu.VMEM((8, ROWS), jnp.int32),
-            pltpu.VMEM((8, ROWS), BF16),
-            pltpu.VMEM((QROWS, QHEADS * HD), BF16),
-            pltpu.VMEM((1, HD), F32),
-            pltpu.SemaphoreType.DMA((4,)),
+        in_specs=[VMEM()] * 2,
+        out_specs=[VMEM()] * 2,
+        out_shape=[
+            jax.ShapeDtypeStruct((EXPERTS * LINES, EXPERTS), BF16),
+            jax.ShapeDtypeStruct((EXPERTS, EXPERTS * LINES), BF16),
         ],
         compiler_params=params(16),
-    )(expert_ids, combine_weight, queries, q_gain, other)
+    )(expert_ids, combine_weight)
 
 
 def dispatch_kernel(*refs):
@@ -440,9 +453,7 @@
 
 def combine_kernel(lines_ref, mixing_ref, hidden_ref, out_ref):
     lines = lines_ref[...].reshape(EXPERTS * LINES, PIECE)
-    mixed = lax.dot_general(
-        mixing_ref[...], lines, (((0,), (0,)), ((), ())), preferred_element_type=F32
-    )
+    mixed = jnp.dot(mixing_ref[...], lines, preferred_element_type=F32)
     for k in range(CHUNKS):
         columns = slice(k * PIECE, (k + 1) * PIECE)
         value = hidden_ref[:, columns] + mixed[k * ROWS : (k + 1) * ROWS, :]
@@ -483,12 +494,10 @@
     own = prep(held(cache), held(new_kv), held(k_gain.reshape(1, HD)))
     first_left, second_right = lax.ppermute(own[0], "x", left), lax.ppermute(own[1], "x", right)
     second_left, first_right = lax.ppermute(own[1], "x", left), lax.ppermute(own[0], "x", right)
-    placing, mixing, qn = route(
-        held(expert_ids.T), held(combine_weight.T), held(queries), held(q_gain.reshape(1, HD)), other
-    )
+    qn = norm_queries(held(queries), held(q_gain.reshape(1, HD)), other)
     other = attend_near(1, place, qn, *own)
-    first_left, second_right, placing, mixing, qn, *other = lax.optimization_barrier(
-        (first_left, second_right, placing, mixing, qn, *other)
+    first_left, second_right, qn, *other = lax.optimization_barrier(
+        (first_left, second_right, qn, *other)
     )
     first, second = lax.ppermute(first_left, "x", left), lax.ppermute(second_right, "x", right)
     mine = attend_near(0, place, qn, *own)
@@ -498,11 +507,16 @@
     far, acc, total = lax.optimization_barrier((far, acc, total))
     mine = attend_far(0, place, qn, acc, total, first, second)
     everyone = ("z", "y", "x", "c")
-    parts = project(place, mine, swap(far), weight)
+    parts = list(project(place, mine, swap(far), weight))
+    expert_ids, combine_weight, parts[0] = lax.optimization_barrier(
+        (expert_ids.T, combine_weight.T, parts[0])
+    )
+    placing, mixing = route(expert_ids, combine_weight)
     for level in range(2):
         if level:
             parts = first_sum(place, parts)
-        moved = [lax.ppermute(parts[k], everyone, around(level, k)) for k in (1, 2, 3)]
+        order = (2, 1, 3) if level else (1, 3, 2)
+        moved = [lax.ppermute(parts[k], everyone, around(level, k)) for k in order]
         parts = [parts[0], *moved]
     hidden, lines = dispatch(parts, residual, norm_gain.reshape(1, WIDTH), placing)
     lines = lax.all_to_all(lines, everyone, split_axis=0, concat_axis=0, tiled=True)

time: 137 us -> 136 us (level)
  waiting for transfers between devices: 16.7 us -> 11.6 us
  blocking collectives: 72.1 us -> 74.9 us
  starting transfers between devices: 22.7 us -> 24.7 us
    ppermute x7, waiting for transfers between devices: 16.7 us -> 11.6 us  [the longest x6 11.5 us: per_device(): moved = [lax.ppermute(parts[k], everyone, around(level, k)) for k in order]]
    all_to_all x2, blocking collectives: 72.1 us -> 74.9 us  [per_device(): lax.all_to_all(lines, everyone, split_axis=0, concat_axis=0, tiled=True)]
    ppermute x7, starting transfers between devices: 13.1 us -> 15.1 us  [the longest x6 12.2 us: per_device(): moved = [lax.ppermute(parts[k], everyone, around(level, k)) for k in order]]
  transfers between devices with their start and end apart: 14 -> 14, of which waited for: 6 -> 4; matrix products, arithmetic and copies ran while one was open for 0% -> 0% of each run, Pallas kernels for 8% -> 9%
where the time goes in v2:
time: 136 us; the launch traced here: 137 us
  blocking collectives  74.9 us (55%)
  starting transfers between devices  24.7 us (18%)
  Pallas kernels  24.3 us (18%)
  waiting for transfers between devices  11.6 us (9%)
    all_to_all x2, blocking collectives, per_device(): lax.all_to_all(lines, everyone, split_axis=0, concat_axis=0, tiled=True)  74.9 us
    ppermute x6, starting transfers between devices, per_device(): moved = [lax.ppermute(parts[k], everyone, around(level, k)) for k in order]  12.2 us
    ppermute x6, waiting for transfers between devices, per_device(): moved = [lax.ppermute(parts[k], everyone, around(level, k)) for k in order]  11.5 us
    pallas_call x1, Pallas kernels, experts(): pl.pallas_call(expert_kernel, in_specs=[VMEM()] * 3, out_specs=VMEM(), ou...  6.26 us
    pallas_call x2, Pallas kernels, attend_near(): pl.pallas_call(functools.partial(near_kernel, who), in_specs=[SMEM()] + [...  3.46 us
    pallas_call x1, Pallas kernels, attend_middle(): pl.pallas_call(middle_kernel, in_specs=[SMEM()] + [VMEM()] * 9 + [HBM()],...  3.01 us
    ppermute x1, starting transfers between devices, per_device(): parts = list(project(place, mine, swap(far), weight))  2.89 us
    pallas_call x2, Pallas kernels, attend_far(): pl.pallas_call(functools.partial(far_kernel, who), in_specs=[SMEM()] + [V...  2.87 us
  transfers between devices with their start and end apart: 14, of which 4 were waited for; matrix products, arithmetic and copies ran while one was open for 0% of the time, Pallas kernels for 9%

profile of v2, /device:TPU:1, one launch (start us, length us, event | category | flops | bytes accessed | tf_op | source)
XLA Modules:
  0.0 136.5 jit_solution(13662583933124607521)
XLA Ops:
  0.0 1.4 %collective-permute-start.2 = (bf16[256,512]{1,0:T(8,128)(2,1)}, bf16[256,512]{1,0:T(8,128)(2,1)S(1)}, u32[]{:S(2)}, u32[]{:S(2)}) collective-permute-start(bf16[256,512]{1,0:T(8,128)(2,1)} %q_ref.1), channel_id=1, source_target_pairs={{0,1},{1,0},{2,3},{3,2},{4,5},{5,4},{6,7},{7,6},{8,9},{9,8},{10,11... | collective-permute-start | bytes 786440 | tf_op jit(solution)/shard_map/ppermute | solution.py:492
  1.4 1.2 shard_map.127
  2.6 1.4 collective-permute-start
  4.0 1.4 %collective-permute-start.1 = (bf16[384,256]{1,0:T(8,128)(2,1)S(1)}, bf16[384,256]{1,0:T(8,128)(2,1)S(1)}, u32[]{:S(2)}, u32[]{:S(2)}) collective-permute-start(bf16[384,256]{1,0:T(8,128)(2,1)S(1)} %get-tuple-element.38.second), channel_id=1, source_target_pairs={{0,6},{2,0},{4,2},{6,4},{1,7},{3,1},{5,3},{7,5},{8,14},{10,8},{12,... | collective-permute-start | bytes 589832 | tf_op jit(solution)/shard_map/ppermute | solution.py:495
  5.5 2.6 %collective-permute-start.4 = (bf16[384,256]{1,0:T(8,128)(2,1)S(1)}, bf16[384,256]{1,0:T(8,128)(2,1)S(1)}, u32[]{:S(2)}, u32[]{:S(2)}) collective-permute-start(bf16[384,256]{1,0:T(8,128)(2,1)S(1)} %get-tuple-element.37.first), channel_id=1, source_target_pairs={{0,6},{2,0},{4,2},{6,4},{1,7},{3,1},{5,3},{7,5},{8,14},{10,8},{12,... | collective-permute-start | bytes 589832 | tf_op jit(solution)/shard_map/ppermute | solution.py:496
  8.8 1.3 shard_map.128.qn
  10.2 1.4 %shard_map.129 = (f32[1024,128]{1,0:T(8,128)S(1)}, f32[1024,128]{1,0:T(8,128)S(1)}) custom-call(s32[5]{0:T(128)S(1)} %stack.19.place_ref, bf16[2,1024,128]{2,1,0:T(8,128)(2,1)S(1)} %shard_map.128.qn, bf16[384,256]{1,0:T(8,128)(2,1)S(1)} %get-tuple-element.37.first, bf16[384,256]{1,0:T(8,128)(2,1)S(1)} %get-tuple-element.38.second), custom_call_target="tpu_custom_call" | custom-call | tf_op jit(solution)/shard_map/pallas_call | solution.py:155
  11.6 2.7 %collective-permute-start.6 = (bf16[384,256]{1,0:T(8,128)(2,1)S(1)}, bf16[384,256]{1,0:T(8,128)(2,1)S(1)}, u32[]{:S(2)}, u32[]{:S(2)}) collective-permute-start(bf16[384,256]{1,0:T(8,128)(2,1)S(1)} %collective-permute-done.1.refs_3_), channel_id=1, source_target_pairs={{0,6},{2,0},{4,2},{6,4},{1,7},{3,1},{5,3},{7,5},{8,14},{10,8},{12,... | collective-permute-start | bytes 589832 | tf_op jit(solution)/shard_map/ppermute | solution.py:502
  14.3 2.1 %shard_map.130 = (f32[1024,128]{1,0:T(8,128)S(1)}, f32[1024,128]{1,0:T(8,128)S(1)}) custom-call(s32[5]{0:T(128)S(1)} %stack.19.place_ref, bf16[2,1024,128]{2,1,0:T(8,128)(2,1)S(1)} %shard_map.128.qn, bf16[384,256]{1,0:T(8,128)(2,1)S(1)} %get-tuple-element.37.first, bf16[384,256]{1,0:T(8,128)(2,1)S(1)} %get-tuple-element.38.second), custom_call_target="tpu_custom_call" | custom-call | tf_op jit(solution)/shard_map/pallas_call | solution.py:155
  16.4 3.0 %shard_map.131 = (f32[2,1024,128]{2,1,0:T(8,128)S(1)}, f32[2,1024,128]{2,1,0:T(8,128)S(1)}, bf16[512,4096]{1,0:T(8,128)(2,1)S(1)}) custom-call(s32[5]{0:T(128)S(1)} %stack.19.place_ref, bf16[2,1024,128]{2,1,0:T(8,128)(2,1)S(1)} %shard_map.128.qn, f32[1024,128]{1,0:T(8,128)S(1)} %get-tuple-element.42.own_acc, f32[1024,128]{1,0:T(8,128)S(1)} %get-tuple-element.43.own_total, ...), custom_call_target="tpu_custom_call" | custom-call | tf_op jit(solution)/shard_map/pallas_call | solution.py:186
  19.5 1.4 %shard_map.132 = bf16[1024,256]{1,0:T(8,128)(2,1)S(1)} custom-call(s32[5]{0:T(128)S(1)} %stack.19.place_ref, bf16[2,1024,128]{2,1,0:T(8,128)(2,1)S(1)} %shard_map.128.qn, f32[2,1024,128]{2,1,0:T(8,128)S(1)} %get-tuple-element.50.acc_ref, f32[2,1024,128]{2,1,0:T(8,128)S(1)} %get-tuple-element.51.total_ref, bf16[384,256]{1,0:T(8,128)(2,1)S(1)} %collective-permute-done.5.first, ...), custom_call_target="tpu_custom_call" | custom-call | tf_op jit(solution)/shard_map/pallas_call | solution.py:206
  20.9 2.9 %collective-permute-start.7 = (bf16[1024,256]{1,0:T(8,128)(2,1)S(1)}, bf16[1024,256]{1,0:T(8,128)(2,1)S(1)}, u32[]{:S(2)}, u32[]{:S(2)}) collective-permute-start(bf16[1024,256]{1,0:T(8,128)(2,1)S(1)} %shard_map.132), channel_id=1, source_target_pairs={{0,1},{1,0},{2,3},{3,2},{4,5},{5,4},{6,7},{7,6},{8,9},{9,8},{10,11... | collective-permute-start | bytes 1572872 | tf_op jit(solution)/shard_map/ppermute | solution.py:510
  23.8 1.4 %shard_map.133.own_ref = f32[1024,256]{1,0:T(8,128)S(1)} custom-call(s32[5]{0:T(128)S(1)} %stack.19.place_ref, bf16[2,1024,128]{2,1,0:T(8,128)(2,1)S(1)} %shard_map.128.qn, f32[2,1024,128]{2,1,0:T(8,128)S(1)} %get-tuple-element.50.acc_ref, f32[2,1024,128]{2,1,0:T(8,128)S(1)} %get-tuple-element.51.total_ref, ...), custom_call_target="tpu_custom_call" | custom-call | tf_op jit(solution)/shard_map/pallas_call | solution.py:206
  25.4 2.0 %shard_map.134 = (bf16[4,16,4096]{2,1,0:T(8,128)(2,1)S(1)}, bf16[4,16,4096]{2,1,0:T(8,128)(2,1)S(1)}, bf16[4,16,4096]{2,1,0:T(8,128)(2,1)S(1)}, bf16[4,16,4096]{2,1,0:T(8,128)(2,1)S(1)}) custom-call(s32[5]{0:T(128)S(1)} %stack.19.place_ref, f32[1024,256]{1,0:T(8,128)S(1)} %shard_map.133.own_ref, bf16[1024,256]{1,0:T(8,128)(2,1)S(1)} %collective-permute-done.7.other_ref, ...), custom_call_target="tpu_custom_call" | custom-call | tf_op jit(solution)/shard_map/pallas_call | solution.py:244
  27.4 3.8 %collective-permute-start.10 = (bf16[4,16,4096]{2,1,0:T(8,128)(2,1)S(1)}, bf16[4,16,4096]{2,1,0:T(8,128)(2,1)S(1)}, u32[]{:S(2)}, u32[]{:S(2)}) collective-permute-start(bf16[4,16,4096]{2,1,0:T(8,128)(2,1)S(1)} %get-tuple-element.58), channel_id=1, source_target_pairs={{0,16},{1,65},{2,18},{3,67},{4,20},{5,69},{6,22},{7,71},{8,24},{9,... | collective-permute-start | bytes 1572872 | tf_op jit(solution)/shard_map/ppermute | solution.py:519
  31.9 1.9 %collective-permute-start.9 = (bf16[4,16,4096]{2,1,0:T(8,128)(2,1)S(1)}, bf16[4,16,4096]{2,1,0:T(8,128)(2,1)S(1)}, u32[]{:S(2)}, u32[]{:S(2)}) collective-permute-start(bf16[4,16,4096]{2,1,0:T(8,128)(2,1)S(1)} %get-tuple-element.57), channel_id=1, source_target_pairs={{0,24},{1,97},{2,26},{3,99},{4,28},{5,101},{6,30},{7,103},{8,0},{9... | collective-permute-start | bytes 1572872 | tf_op jit(solution)/shard_map/ppermute | solution.py:519
  33.8 4.2 %collective-permute-done.10.refs_3_ = bf16[4,16,4096]{2,1,0:T(8,128)(2,1)S(1)} collective-permute-done((bf16[4,16,4096]{2,1,0:T(8,128)(2,1)S(1)}, bf16[4,16,4096]{2,1,0:T(8,128)(2,1)S(1)}, u32[]{:S(2)}, u32[]{:S(2)}) %collective-permute-start.10) | collective-permute-done | bytes 524320 | tf_op jit(solution)/shard_map/ppermute | solution.py:519
  38.1 5.6 %collective-permute-done.8.refs_1_ = bf16[4,16,4096]{2,1,0:T(8,128)(2,1)S(1)} collective-permute-done((bf16[4,16,4096]{2,1,0:T(8,128)(2,1)S(1)}, bf16[4,16,4096]{2,1,0:T(8,128)(2,1)S(1)}, u32[]{:S(2)}, u32[]{:S(2)}) %collective-permute-start.8) | collective-permute-done | bytes 524320 | tf_op jit(solution)/shard_map/ppermute | solution.py:519
  45.2 3.1 %collective-permute-start.11 = (bf16[16,4096]{1,0:T(8,128)(2,1)S(1)}, bf16[16,4096]{1,0:T(8,128)(2,1)S(1)}, u32[]{:S(2)}, u32[]{:S(2)}) collective-permute-start(bf16[16,4096]{1,0:T(8,128)(2,1)S(1)} %get-tuple-element.60), channel_id=1, source_target_pairs={{0,64},{1,17},{2,66},{3,19},{4,68},{5,21},{6,70},{7,23},{8,72},{9,... | collective-permute-start | bytes 393224 | tf_op jit(solution)/shard_map/ppermute | solution.py:519
  48.7 2.3 %collective-permute-start.13 = (bf16[16,4096]{1,0:T(8,128)(2,1)S(1)}, bf16[16,4096]{1,0:T(8,128)(2,1)S(1)}, u32[]{:S(2)}, u32[]{:S(2)}) collective-permute-start(bf16[16,4096]{1,0:T(8,128)(2,1)S(1)} %get-tuple-element.62), channel_id=1, source_target_pairs={{0,96},{1,25},{2,98},{3,27},{4,100},{5,29},{6,102},{7,31},{8,104},... | collective-permute-start | bytes 393224 | tf_op jit(solution)/shard_map/ppermute | solution.py:519
  50.9 1.2 shard_map.136
  54.2 40.5 %all_to_all.10.lines_ref = bf16[128,16,512]{2,1,0:T(8,128)(2,1)S(1)} all-to-all(bf16[128,16,512]{2,1,0:T(8,128)(2,1)S(1)} %get-tuple-element.66), channel_id=1, replica_groups=mesh['z'=4,'y'=4,'x'=4,'c'=2] {'z','y','x','c'}, dimensions={0} | all-to-all | bytes 4194304 | tf_op jit(solution)/shard_map/all_to_all | solution.py:522
  94.8 6.3 %shard_map.138 = bf16[128,16,512]{2,1,0:T(8,128)(2,1)S(1)} custom-call(bf16[128,16,512]{2,1,0:T(8,128)(2,1)S(1)} %all_to_all.10.lines_ref, bf16[4096,1536]{1,0:T(8,128)(2,1)S(1)} %bitcast.13, bf16[768,4096]{1,0:T(8,128)(2,1)S(1)} %bitcast.16), custom_call_target="tpu_custom_call" | custom-call | tf_op jit(solution)/shard_map/pallas_call | solution.py:439
  101.1 34.4 %all_to_all.11.lines_ref = bf16[128,16,512]{2,1,0:T(8,128)(2,1)S(1)} all-to-all(bf16[128,16,512]{2,1,0:T(8,128)(2,1)S(1)} %shard_map.138), channel_id=1, replica_groups=mesh['z'=4,'y'=4,'x'=4,'c'=2] {'z','y','x','c'}, dimensions={0} | all-to-all | bytes 4194304 | tf_op jit(solution)/shard_map/all_to_all | solution.py:524
  (40 shorter events, 6.2 us)
Async XLA Ops:
  0.0 8.8 %collective-permute-start.2 = (bf16[256,512]{1,0:T(8,128)(2,1)}, bf16[256,512]{1,0:T(8,128)(2,1)S(1)}, u32[]{:S(2)}, u32[]{:S(2)}) collective-permute-start(bf16[256,512]{1,0:T(8,128)(2,1)} %q_ref.1), channel_id=1, source_target_pairs={{0,1},{1,0},{2,3},{3,2},{4,5},{5,4},{6,7},{7,6},{8,9},{9,8},{10,11... | collective-permute-start | bytes 786440 | tf_op jit(solution)/shard_map/ppermute | solution.py:492
  2.6 8.9 %collective-permute-start = (bf16[384,256]{1,0:T(8,128)(2,1)S(1)}, bf16[384,256]{1,0:T(8,128)(2,1)S(1)}, u32[]{:S(2)}, u32[]{:S(2)}) collective-permute-start(bf16[384,256]{1,0:T(8,128)(2,1)S(1)} %get-tuple-element.37.first), channel_id=1, source_target_pairs={{0,2},{2,4},{4,6},{6,0},{1,3},{3,5},{5,7},{7,1},{8,10},{10,12},{12... | collective-permute-start | bytes 589832 | tf_op jit(solution)/shard_map/ppermute | solution.py:495
  4.0 7.5 %collective-permute-start.1 = (bf16[384,256]{1,0:T(8,128)(2,1)S(1)}, bf16[384,256]{1,0:T(8,128)(2,1)S(1)}, u32[]{:S(2)}, u32[]{:S(2)}) collective-permute-start(bf16[384,256]{1,0:T(8,128)(2,1)S(1)} %get-tuple-element.38.second), channel_id=1, source_target_pairs={{0,6},{2,0},{4,2},{6,4},{1,7},{3,1},{5,3},{7,5},{8,14},{10,8},{12,... | collective-permute-start | bytes 589832 | tf_op jit(solution)/shard_map/ppermute | solution.py:495
  5.4 11.0 %collective-permute-start.3 = (bf16[384,256]{1,0:T(8,128)(2,1)S(1)}, bf16[384,256]{1,0:T(8,128)(2,1)S(1)}, u32[]{:S(2)}, u32[]{:S(2)}) collective-permute-start(bf16[384,256]{1,0:T(8,128)(2,1)S(1)} %get-tuple-element.38.second), channel_id=1, source_target_pairs={{0,2},{2,4},{4,6},{6,0},{1,3},{3,5},{5,7},{7,1},{8,10},{10,12},{12... | collective-permute-start | bytes 589832 | tf_op jit(solution)/shard_map/ppermute | solution.py:496
  5.5 10.9 %collective-permute-start.4 = (bf16[384,256]{1,0:T(8,128)(2,1)S(1)}, bf16[384,256]{1,0:T(8,128)(2,1)S(1)}, u32[]{:S(2)}, u32[]{:S(2)}) collective-permute-start(bf16[384,256]{1,0:T(8,128)(2,1)S(1)} %get-tuple-element.37.first), channel_id=1, source_target_pairs={{0,6},{2,0},{4,2},{6,4},{1,7},{3,1},{5,3},{7,5},{8,14},{10,8},{12,... | collective-permute-start | bytes 589832 | tf_op jit(solution)/shard_map/ppermute | solution.py:496
  11.6 7.9 %collective-permute-start.5 = (bf16[384,256]{1,0:T(8,128)(2,1)S(1)}, bf16[384,256]{1,0:T(8,128)(2,1)S(1)}, u32[]{:S(2)}, u32[]{:S(2)}) collective-permute-start(bf16[384,256]{1,0:T(8,128)(2,1)S(1)} %collective-permute-done.refs_0_), channel_id=1, source_target_pairs={{0,2},{2,4},{4,6},{6,0},{1,3},{3,5},{5,7},{7,1},{8,10},{10,12},{12... | collective-permute-start | bytes 589832 | tf_op jit(solution)/shard_map/ppermute | solution.py:502
  11.6 7.8 %collective-permute-start.6 = (bf16[384,256]{1,0:T(8,128)(2,1)S(1)}, bf16[384,256]{1,0:T(8,128)(2,1)S(1)}, u32[]{:S(2)}, u32[]{:S(2)}) collective-permute-start(bf16[384,256]{1,0:T(8,128)(2,1)S(1)} %collective-permute-done.1.refs_3_), channel_id=1, source_target_pairs={{0,6},{2,0},{4,2},{6,4},{1,7},{3,1},{5,3},{7,5},{8,14},{10,8},{12,... | collective-permute-start | bytes 589832 | tf_op jit(solution)/shard_map/ppermute | solution.py:502
  16.4 78.3 %slice-start = ((s8[12582912]{0:T(1024)(128)(4,1)}), s8[4194304]{0:T(1024)(128)(4,1)S(1)}, s32[]{:S(2)}) async-start(s8[12582912]{0:T(1024)(128)(4,1)} %bitcast.11), calls=%async_computation.2 | async-start | bytes 8388608
  19.5 75.3 %slice-start.1 = ((s8[12582912]{0:T(1024)(128)(4,1)}), s8[4194304]{0:T(1024)(128)(4,1)S(1)}, s32[]{:S(2)}) async-start(s8[12582912]{0:T(1024)(128)(4,1)} %bitcast.11), calls=%async_computation.3 | async-start | bytes 8388608
  20.9 4.4 %collective-permute-start.7 = (bf16[1024,256]{1,0:T(8,128)(2,1)S(1)}, bf16[1024,256]{1,0:T(8,128)(2,1)S(1)}, u32[]{:S(2)}, u32[]{:S(2)}) collective-permute-start(bf16[1024,256]{1,0:T(8,128)(2,1)S(1)} %shard_map.132), channel_id=1, source_target_pairs={{0,1},{1,0},{2,3},{3,2},{4,5},{5,4},{6,7},{7,6},{8,9},{9,8},{10,11... | collective-permute-start | bytes 1572872 | tf_op jit(solution)/shard_map/ppermute | solution.py:510
  23.8 70.9 %slice-start.3 = ((s8[6291456]{0:T(1024)(128)(4,1)}), s8[4194304]{0:T(1024)(128)(4,1)S(1)}, s32[]{:S(2)}) async-start(s8[6291456]{0:T(1024)(128)(4,1)} %bitcast.14), calls=%async_computation.5 | async-start | bytes 8388608
  25.3 25.7 %copy-start.2 = (s32[16,8]{0,1:T(8,128)S(1)}, s32[16,8]{0,1:T(8,128)}, u32[]{:S(2)}) copy-start(s32[16,8]{0,1:T(8,128)} %param.21) | copy-start | bytes 1540
  25.3 25.7 %copy-start.3 = (bf16[16,8]{0,1:T(8,128)(2,1)S(1)}, bf16[16,8]{0,1:T(8,128)(2,1)}, u32[]{:S(2)}) copy-start(bf16[16,8]{0,1:T(8,128)(2,1)} %param.22) | copy-start | bytes 772
  25.3 28.0 %copy-start = (bf16[16,4096]{1,0:T(8,128)(2,1)S(1)}, bf16[16,4096]{1,0:T(8,128)(2,1)}, u32[]{:S(2)}) copy-start(bf16[16,4096]{1,0:T(8,128)(2,1)} %refs_4_.3) | copy-start | bytes 393220
  25.3 28.0 %copy-start.1 = (f32[4096]{0:T(1024)S(1)}, f32[4096]{0:T(1024)}, u32[]{:S(2)}) copy-start(f32[4096]{0:T(1024)} %param.20) | copy-start | bytes 49156
  25.4 69.4 %slice-start.2 = ((s8[12582912]{0:T(1024)(128)(4,1)}), s8[4194304]{0:T(1024)(128)(4,1)S(1)}, s32[]{:S(2)}) async-start(s8[12582912]{0:T(1024)(128)(4,1)} %bitcast.11), calls=%async_computation.4 | async-start | bytes 8388608
  25.4 69.4 %slice-start.4 = ((s8[6291456]{0:T(1024)(128)(4,1)}), s8[2097152]{0:T(1024)(128)(4,1)S(1)}, s32[]{:S(2)}) async-start(s8[6291456]{0:T(1024)(128)(4,1)} %bitcast.14), calls=%async_computation.6 | async-start | bytes 4194304
  27.4 10.7 %collective-permute-start.10 = (bf16[4,16,4096]{2,1,0:T(8,128)(2,1)S(1)}, bf16[4,16,4096]{2,1,0:T(8,128)(2,1)S(1)}, u32[]{:S(2)}, u32[]{:S(2)}) collective-permute-start(bf16[4,16,4096]{2,1,0:T(8,128)(2,1)S(1)} %get-tuple-element.58), channel_id=1, source_target_pairs={{0,16},{1,65},{2,18},{3,67},{4,20},{5,69},{6,22},{7,71},{8,24},{9,... | collective-permute-start | bytes 1572872 | tf_op jit(solution)/shard_map/ppermute | solution.py:519
  31.2 12.5 %collective-permute-start.8 = (bf16[4,16,4096]{2,1,0:T(8,128)(2,1)S(1)}, bf16[4,16,4096]{2,1,0:T(8,128)(2,1)S(1)}, u32[]{:S(2)}, u32[]{:S(2)}) collective-permute-start(bf16[4,16,4096]{2,1,0:T(8,128)(2,1)S(1)} %get-tuple-element.56), channel_id=1, source_target_pairs={{0,8},{1,33},{2,10},{3,35},{4,12},{5,37},{6,14},{7,39},{8,16},{9,4... | collective-permute-start | bytes 1572872 | tf_op jit(solution)/shard_map/ppermute | solution.py:519
  31.9 12.3 %collective-permute-start.9 = (bf16[4,16,4096]{2,1,0:T(8,128)(2,1)S(1)}, bf16[4,16,4096]{2,1,0:T(8,128)(2,1)S(1)}, u32[]{:S(2)}, u32[]{:S(2)}) collective-permute-start(bf16[4,16,4096]{2,1,0:T(8,128)(2,1)S(1)} %get-tuple-element.57), channel_id=1, source_target_pairs={{0,24},{1,97},{2,26},{3,99},{4,28},{5,101},{6,30},{7,103},{8,0},{9... | collective-permute-start | bytes 1572872 | tf_op jit(solution)/shard_map/ppermute | solution.py:519
  45.2 7.0 %collective-permute-start.11 = (bf16[16,4096]{1,0:T(8,128)(2,1)S(1)}, bf16[16,4096]{1,0:T(8,128)(2,1)S(1)}, u32[]{:S(2)}, u32[]{:S(2)}) collective-permute-start(bf16[16,4096]{1,0:T(8,128)(2,1)S(1)} %get-tuple-element.60), channel_id=1, source_target_pairs={{0,64},{1,17},{2,66},{3,19},{4,68},{5,21},{6,70},{7,23},{8,72},{9,... | collective-permute-start | bytes 393224 | tf_op jit(solution)/shard_map/ppermute | solution.py:519
  48.3 5.0 %collective-permute-start.12 = (bf16[16,4096]{1,0:T(8,128)(2,1)S(1)}, bf16[16,4096]{1,0:T(8,128)(2,1)S(1)}, u32[]{:S(2)}, u32[]{:S(2)}) collective-permute-start(bf16[16,4096]{1,0:T(8,128)(2,1)S(1)} %get-tuple-element.61), channel_id=1, source_target_pairs={{0,32},{1,9},{2,34},{3,11},{4,36},{5,13},{6,38},{7,15},{8,40},{9,1... | collective-permute-start | bytes 393224 | tf_op jit(solution)/shard_map/ppermute | solution.py:519
  48.7 4.6 %collective-permute-start.13 = (bf16[16,4096]{1,0:T(8,128)(2,1)S(1)}, bf16[16,4096]{1,0:T(8,128)(2,1)S(1)}, u32[]{:S(2)}, u32[]{:S(2)}) collective-permute-start(bf16[16,4096]{1,0:T(8,128)(2,1)S(1)} %get-tuple-element.62), channel_id=1, source_target_pairs={{0,96},{1,25},{2,98},{3,27},{4,100},{5,29},{6,102},{7,31},{8,104},... | collective-permute-start | bytes 393224 | tf_op jit(solution)/shard_map/ppermute | solution.py:519
